TPU v7x, 128 devices: a whole 4x4x4 slice. The times are simulated.
128 devices in a mesh: blk: 32 (over x, z, y_lo), pre: 4 (over y_hi, core).
Axes of the slice: x: 4, y: 4 (y_hi: 2, y_lo: 2; y = y_hi * 2 + y_lo), z: 4, core: 2. Of those that a mesh axis runs over, the one named last changes fastest.
Arguments:
- record: bfloat16 [4096, 131072], P('blk', 'pre'), may hold values from -6 to 6
- quality: int32 [4096], P('blk'), may hold values 0 or 1
Outputs:
- stacks: float32 [4, 4, 64, 4096, 128], P('pre', None, None, 'blk')
All inputs are finite; a program needn't handle non-finite values. No bound on the sum of `quality` on one device may be relied on, other than what follows from the above.
Results may differ from a plain program's by a relative error of at most 0.0048.
Values may be sent and summed in bfloat16 or wider, within the bound.
A program may use at most 128 MiB of HBM per device.

v0:
```python
import math

import jax
import jax.numpy as jnp
import ml_dtypes
import numpy as np
from jax import lax
from jax.experimental import pallas as pl
from jax.experimental.pallas import tpu as pltpu
from jax.sharding import PartitionSpec as P

M = 512
R = 4
KT = 16
FB = 128
NLAG = 64
BAND0 = 16
CH = 128
HALF = 1024
FRAMES = 32
GROUPS = 32
ROWS = (GROUPS + 2) * 8
HALO = HALF + 128
NT = (((1,), (1,)), ((), ()))
BF = jnp.bfloat16
F32 = jnp.float32


def filter_taps():
    index = np.arange(KT, dtype=np.float32)
    centre = np.float32((KT - 1) / 2.0)
    shaped = np.sinc((index - centre) / np.float32(R)) * (
        0.54 - 0.46 * np.cos(2.0 * math.pi * index / (KT - 1))
    )
    return (shaped / np.sum(shaped)).astype(np.float32).astype(ml_dtypes.bfloat16)


def split(table):
    high = table.astype(np.float32).astype(ml_dtypes.bfloat16)
    low = (table - high.astype(np.float64)).astype(np.float32).astype(ml_dtypes.bfloat16)
    return high, low


def half_tables():
    taps = filter_taps().astype(np.float64)
    toeplitz = np.zeros((M // 2, HALF + 128))
    for m in range(M // 2):
        toeplitz[m, R * m : R * m + KT] = taps
    group = np.arange(-1, GROUPS + 1)
    bins = BAND0 + group[:, None] + 32 * np.arange(4)[None, :]
    phase = 2.0 * math.pi * ((bins[:, :, None] * np.arange(M // 2)) % M) / M
    both = np.stack([np.cos(phase), -np.sin(phase)], 1).reshape(ROWS, M // 2)
    table = both @ toeplitz
    high, low = split(table)
    main = np.concatenate([high[:, :HALF], low[:, :HALF]], 0)
    tail = np.concatenate([high[:, HALF:], low[:, HALF:]], 1)
    return main, tail


def lag_table():
    lags = np.arange(NLAG) - NLAG // 2
    bins = (BAND0 + np.arange(GROUPS)[:, None, None] + 32 * np.arange(4)[None, None, :])
    phase = 2.0 * math.pi * (((lags[:, None, None, None] + M) * bins[None]) % M) / M
    both = np.concatenate([np.cos(phase), -np.sin(phase)], 2).reshape(NLAG, 2 * FB)
    rounded = both.astype(np.float32).astype(ml_dtypes.bfloat16).astype(np.float32)
    return (rounded / 64.0).astype(ml_dtypes.bfloat16)


def spread_table():
    table = np.zeros((CH, 2, 4, 2, CH), np.float32)
    for c in range(CH):
        for o in range(2):
            table[c, o, :, o, c] = 1.0
    return table.reshape(CH * 8, 2 * CH).astype(ml_dtypes.bfloat16)


def spectra_kernel(main_ref, tail_ref, quality_ref, first_ref, one_ref, two_ref, three_ref, halo_ref,
                   white_ref, turned_ref, held):
    step = pl.program_id(0)
    last = step == FRAMES // 2 - 1

    def transform(raw, after):
        both = lax.dot_general(main_ref[...], raw, NT, preferred_element_type=F32)
        ends = jnp.concatenate([after, after], 1)
        return (both[:ROWS] + both[ROWS:]) + lax.dot_general(
            tail_ref[...], ends, NT, preferred_element_type=F32)

    @pl.when(step == 0)
    def _():
        held[...] = transform(first_ref[...], one_ref[:, :128]).reshape(GROUPS + 2, 8, CH)

    two = jnp.where(last, halo_ref[:, :HALF], two_ref[...])
    three = jnp.where(last, halo_ref[:, HALF:], three_ref[...])
    raw = jnp.concatenate([one_ref[...], two], 0)
    after = jnp.concatenate([two[:, :128], three], 0)
    pair = transform(raw, after)
    zero = held[...]
    first = pair[:, :CH].reshape(GROUPS + 2, 8, CH)
    second = pair[:, CH:].reshape(GROUPS + 2, 8, CH)
    held[...] = second
    group = lax.broadcasted_iota(jnp.int32, (GROUPS, 8, CH), 0)
    odd = (group % 2) == 1
    row = lax.broadcasted_iota(jnp.int32, (GROUPS, 8, CH), 1)
    keep = quality_ref[...].reshape(1, 1, CH)

    def whiten(front, back):
        side = 0.25 * (front[:GROUPS] + front[2:])
        spec = 0.5 * front[1 : GROUPS + 1] - side
        other = 0.5 * back[1 : GROUPS + 1] + 0.25 * (back[:GROUPS] + back[2:])
        spec = spec + jnp.where(odd, -other, other)
        square = spec * spec
        level = jnp.sum(jnp.sum(square, 0), 0, keepdims=True).reshape(1, 1, CH) * (1.0 / FB)
        power = square + pltpu.roll(square, 4, 1)
        white = spec * lax.rsqrt(power + (0.1 * level + 1e-06)) * keep
        turned = pltpu.roll(white, 4, 1)
        return white, jnp.where(row < 4, turned, -turned)

    w0, t0 = whiten(zero, first)
    w1, t1 = whiten(first, second)
    white_ref[...] = jnp.concatenate([w0, w1], 1).astype(BF)
    turned_ref[...] = jnp.concatenate([t0, t1], 1).astype(BF)


def spectra(record, halo, quality):
    main, tail = half_tables()
    keep = quality.astype(F32).reshape(1, CH)
    whole = lambda *shape: pl.BlockSpec(shape, lambda i: (0,) * len(shape))
    out = jax.ShapeDtypeStruct((GROUPS, FRAMES * 8, CH), BF)
    return pl.pallas_call(
        spectra_kernel,
        grid=(FRAMES // 2,),
        out_shape=(out, out),
        in_specs=[
            whole(2 * ROWS, HALF),
            whole(ROWS, 256),
            whole(1, CH),
            pl.BlockSpec((CH, HALF), lambda i: (0, 0)),
            pl.BlockSpec((CH, HALF), lambda i: (0, 2 * i + 1)),
            pl.BlockSpec((CH, HALF), lambda i: (0, jnp.minimum(2 * i + 2, FRAMES - 1))),
            pl.BlockSpec((CH, 128), lambda i: (0, jnp.minimum((2 * i + 3) * 8, FRAMES * 8 - 1))),
            whole(CH, HALO),
        ],
        out_specs=[pl.BlockSpec((GROUPS, 16, CH), lambda i: (0, i, 0))] * 2,
        scratch_shapes=[pltpu.VMEM((GROUPS + 2, 8, CH), F32)],
        compiler_params=pltpu.CompilerParams(vmem_limit_bytes=40 * 2**20),
        name="spectra",
    )(jnp.asarray(main), jnp.asarray(tail), keep, record, record, record, record, halo)


CBLK = 32


def correlate_kernel(spread_ref, lag_ref, white_ref, turned_ref, p1_ref, p2_ref, p3_ref, out_ref, cross):
    rows = lax.broadcasted_iota(jnp.int32, (CBLK * 8, 256), 0)
    cols = lax.broadcasted_iota(jnp.int32, (CBLK * 8, 256), 1)
    diagonal = (rows % 4) == (cols % 4)

    def stage(group):
        own = jnp.concatenate([white_ref[group], turned_ref[group]], 1)
        left = lax.dot_general(spread_ref[...], own, NT, preferred_element_type=F32)
        left = jnp.where(diagonal, left, 0.0).astype(BF)
        right = jnp.concatenate([white_ref[group], p1_ref[group], p2_ref[group], p3_ref[group]], 1)
        return jnp.dot(left, right, preferred_element_type=F32).reshape(CBLK, 8, 4 * CH)

    @pl.loop(0, GROUPS // 2)
    def _(pair):
        both = jnp.concatenate([stage(2 * pair), stage(2 * pair + 1)], 1)
        cross[:, pl.ds(pl.multiple_of(pair * 16, 16), 16), :] = both.astype(BF)

    @pl.loop(0, CBLK)
    def _(c):
        result = jnp.dot(lag_ref[...], cross[c], preferred_element_type=F32)
        for d in range(4):
            flat = out_ref.at[d].reshape(NLAG * CBLK, CH)
            flat[pl.ds(c, NLAG, stride=CBLK), :] = result[:, d * CH : (d + 1) * CH]


def correlate(white, turned, partners):
    whole = lambda *shape: pl.BlockSpec(shape, lambda i: (0,) * len(shape))
    spectrum = whole(GROUPS, 256, CH)
    return pl.pallas_call(
        correlate_kernel,
        grid=(CH // CBLK,),
        out_shape=jax.ShapeDtypeStruct((4, NLAG, CH, CH), F32),
        in_specs=[pl.BlockSpec((CBLK * 8, 256), lambda i: (i, 0)), whole(NLAG, 256)] + [spectrum] * 5,
        out_specs=pl.BlockSpec((4, NLAG, CBLK, CH), lambda i: (0, 0, i, 0)),
        scratch_shapes=[pltpu.VMEM((CBLK, 256, 4 * CH), BF)],
        compiler_params=pltpu.CompilerParams(vmem_limit_bytes=60 * 2**20),
        name="correlate",
    )(jnp.asarray(spread_table()), jnp.asarray(lag_table()), white, turned, *partners)


def shards(record, quality):
    count = lax.axis_size("pre")
    halo = lax.ppermute(record[:, :HALO], "pre", [(i, i - 1) for i in range(1, count)])
    white, turned = spectra(record, halo, quality)
    blocks = lax.axis_size("blk")
    partners = [
        lax.ppermute(white, "blk", [(i, (i + d) % blocks) for i in range(blocks)]) for d in range(1, 4)
    ]
    return correlate(white, turned, partners)[None]


def solution(mesh):
    placed = (P("blk", "pre"), P("blk"))
    return jax.shard_map(
        shards,
        mesh=mesh,
        in_specs=placed,
        out_specs=P("pre", None, None, "blk", None),
        check_vma=False,
    )
```

profile of v0, /device:TPU:16, one launch (start us, length us, event | category | flops | bytes accessed | tf_op | source)
XLA Modules:
  0.0 245.5 jit_solution(1254962091952858085)
XLA Ops:
  0.0 1.0 slice.3
  1.0 1.9 collective-permute-start
  2.9 0.7 convert_bitcast_fusion.quality_ref
  3.6 3.6 %collective-permute-done.halo_ref = bf16[128,1152]{1,0:T(8,128)(2,1)S(1)} collective-permute-done((bf16[128,1152]{1,0:T(8,128)(2,1)S(1)}, bf16[128,1152]{1,0:T(8,128)(2,1)S(1)}, u32[]{:S(2)}, u32[]{:S(2)}) %collective-permute-start) | collective-permute-done | bytes 294944 | tf_op jit(solution)/shard_map/ppermute | solution.py:195
  7.1 0.0 copy-start
  7.1 3.4 %copy-done = bf16[128,32768]{1,0:T(8,128)(2,1)S(1)} copy-done((bf16[128,32768]{1,0:T(8,128)(2,1)S(1)}, bf16[128,32768]{1,0:T(8,128)(2,1)}, u32[]{:S(2)}) %copy-start) | copy-done | bytes 8388632
  10.5 0.0 copy-start.3
  10.5 1.2 copy-done.3
  11.8 0.0 copy-start.4
  11.8 0.9 copy-done.4
  12.7 13.3 %spectra.1 = (bf16[32,256,128]{2,1,0:T(8,128)(2,1)S(1)}, bf16[32,256,128]{2,1,0:T(8,128)(2,1)S(1)}) custom-call(bf16[544,1024]{1,0:T(8,128)(2,1)S(1)} %copy-done.3, bf16[272,256]{1,0:T(8,128)(2,1)S(1)} %copy-done.4, f32[1,128]{1,0:T(1,128)S(1)} %convert_bitcast_fusion.quality_ref, bf16[128,32768]{1,0:T(8,128)(2,1)S(1)} %copy-done, ...), custom_call_target="tpu_custom_call" | custom-call | tf_op jit(solution)/shard_map/spectra/pallas_call | solution.py:129
  26.0 0.0 copy-start.2
  26.0 1.3 copy-done.2
  27.3 0.0 copy-start.1
  27.3 3.3 %collective-permute-start.3 = (bf16[32,256,128]{2,1,0:T(8,128)(2,1)S(1)}, bf16[32,256,128]{2,1,0:T(8,128)(2,1)S(1)}, u32[]{:S(2)}, u32[]{:S(2)}) collective-permute-start(bf16[32,256,128]{2,1,0:T(8,128)(2,1)S(1)} %get-tuple-element.7.white_ref), channel_id=1, source_target_pairs={{0,12},{4,16},{8,20},{12,24},{16,28},{20,32},{24,36},{28,40},{32,4... | collective-permute-start | bytes 6291464 | tf_op jit(solution)/shard_map/ppermute | solution.py:199
  30.6 1.9 collective-permute-start.2
  32.5 1.1 collective-permute-start.1
  33.6 46.6 %collective-permute-done.3.p3_ref = bf16[32,256,128]{2,1,0:T(8,128)(2,1)S(1)} collective-permute-done((bf16[32,256,128]{2,1,0:T(8,128)(2,1)S(1)}, bf16[32,256,128]{2,1,0:T(8,128)(2,1)S(1)}, u32[]{:S(2)}, u32[]{:S(2)}) %collective-permute-start.3) | collective-permute-done | bytes 2097184 | tf_op jit(solution)/shard_map/ppermute | solution.py:199
  80.3 0.0 copy-start.5
  80.3 83.7 %collective-permute-done.2.p2_ref = bf16[32,256,128]{2,1,0:T(8,128)(2,1)S(1)} collective-permute-done((bf16[32,256,128]{2,1,0:T(8,128)(2,1)S(1)}, bf16[32,256,128]{2,1,0:T(8,128)(2,1)S(1)}, u32[]{:S(2)}, u32[]{:S(2)}) %collective-permute-start.2) | collective-permute-done | bytes 2097184 | tf_op jit(solution)/shard_map/ppermute | solution.py:199
  164.0 0.0 copy-start.6
  164.0 3.8 %collective-permute-done.1.p1_ref = bf16[32,256,128]{2,1,0:T(8,128)(2,1)S(1)} collective-permute-done((bf16[32,256,128]{2,1,0:T(8,128)(2,1)S(1)}, bf16[32,256,128]{2,1,0:T(8,128)(2,1)S(1)}, u32[]{:S(2)}, u32[]{:S(2)}) %collective-permute-start.1) | collective-permute-done | bytes 2097184 | tf_op jit(solution)/shard_map/ppermute | solution.py:199
  167.7 0.0 copy-done.5
  167.7 0.0 copy-done.6
  167.7 0.0 copy-start.7
  167.7 1.3 copy-done.7
  169.0 0.0 copy-done.1
  169.1 76.5 %correlate.1 = f32[4,64,128,128]{3,2,1,0:T(8,128)} custom-call(bf16[1024,256]{1,0:T(8,128)(2,1)} %constant.10.clone.spread_ref, bf16[64,256]{1,0:T(8,128)(2,1)} %constant.11.clone.lag_ref, bf16[32,256,128]{2,1,0:T(8,128)(2,1)} %copy-done.1, bf16[32,256,128]{2,1,0:T(8,128)(2,1)} %copy-done.2, bf16[32,256,128]{2,1,0:T(8,128)(2,1)} %copy-done.7, ...), custom_call_target="tpu_custom_call" | custom-call | tf_op jit(solution)/shard_map/correlate/pallas_call | solution.py:181
Async XLA Ops:
  1.0 6.1 %collective-permute-start = (bf16[128,1152]{1,0:T(8,128)(2,1)S(1)}, bf16[128,1152]{1,0:T(8,128)(2,1)S(1)}, u32[]{:S(2)}, u32[]{:S(2)}) collective-permute-start(bf16[128,1152]{1,0:T(8,128)(2,1)S(1)} %slice.3), channel_id=1, source_target_pairs={{1,0},{2,1},{3,2},{5,4},{6,5},{7,6},{9,8},{10,9},{11,10},{13,12},{... | collective-permute-start | bytes 884744 | tf_op jit(solution)/shard_map/ppermute | solution.py:195
  7.1 3.4 %copy-start = (bf16[128,32768]{1,0:T(8,128)(2,1)S(1)}, bf16[128,32768]{1,0:T(8,128)(2,1)}, u32[]{:S(2)}) copy-start(bf16[128,32768]{1,0:T(8,128)(2,1)} %three_ref.1) | copy-start | bytes 25165828
  10.5 1.2 copy-start.3
  11.8 0.9 copy-start.4
  26.0 1.3 copy-start.2
  27.3 141.8 %copy-start.1 = (bf16[32,256,128]{2,1,0:T(8,128)(2,1)}, bf16[32,256,128]{2,1,0:T(8,128)(2,1)S(1)}, u32[]{:S(2)}) copy-start(bf16[32,256,128]{2,1,0:T(8,128)(2,1)S(1)} %get-tuple-element.7.white_ref) | copy-start | bytes 6291460
  27.3 53.0 %collective-permute-start.3 = (bf16[32,256,128]{2,1,0:T(8,128)(2,1)S(1)}, bf16[32,256,128]{2,1,0:T(8,128)(2,1)S(1)}, u32[]{:S(2)}, u32[]{:S(2)}) collective-permute-start(bf16[32,256,128]{2,1,0:T(8,128)(2,1)S(1)} %get-tuple-element.7.white_ref), channel_id=1, source_target_pairs={{0,12},{4,16},{8,20},{12,24},{16,28},{20,32},{24,36},{28,40},{32,4... | collective-permute-start | bytes 6291464 | tf_op jit(solution)/shard_map/ppermute | solution.py:199
  30.6 133.4 %collective-permute-start.2 = (bf16[32,256,128]{2,1,0:T(8,128)(2,1)S(1)}, bf16[32,256,128]{2,1,0:T(8,128)(2,1)S(1)}, u32[]{:S(2)}, u32[]{:S(2)}) collective-permute-start(bf16[32,256,128]{2,1,0:T(8,128)(2,1)S(1)} %get-tuple-element.7.white_ref), channel_id=1, source_target_pairs={{0,8},{4,12},{8,16},{12,20},{16,24},{20,28},{24,32},{28,36},{32,40... | collective-permute-start | bytes 6291464 | tf_op jit(solution)/shard_map/ppermute | solution.py:199
  32.5 135.2 %collective-permute-start.1 = (bf16[32,256,128]{2,1,0:T(8,128)(2,1)S(1)}, bf16[32,256,128]{2,1,0:T(8,128)(2,1)S(1)}, u32[]{:S(2)}, u32[]{:S(2)}) collective-permute-start(bf16[32,256,128]{2,1,0:T(8,128)(2,1)S(1)} %get-tuple-element.7.white_ref), channel_id=1, source_target_pairs={{0,4},{4,8},{8,12},{12,16},{16,20},{20,24},{24,28},{28,32},{32,36}... | collective-permute-start | bytes 6291464 | tf_op jit(solution)/shard_map/ppermute | solution.py:199
  80.3 87.5 %copy-start.5 = (bf16[32,256,128]{2,1,0:T(8,128)(2,1)}, bf16[32,256,128]{2,1,0:T(8,128)(2,1)S(1)}, u32[]{:S(2)}) copy-start(bf16[32,256,128]{2,1,0:T(8,128)(2,1)S(1)} %collective-permute-done.3.p3_ref) | copy-start | bytes 6291460
  164.0 3.8 %copy-start.6 = (bf16[32,256,128]{2,1,0:T(8,128)(2,1)}, bf16[32,256,128]{2,1,0:T(8,128)(2,1)S(1)}, u32[]{:S(2)}) copy-start(bf16[32,256,128]{2,1,0:T(8,128)(2,1)S(1)} %collective-permute-done.2.p2_ref) | copy-start | bytes 6291460
  167.7 1.3 copy-start.7
where the time goes:
time: 247 us; the launch traced here: 246 us
  waiting for transfers between devices  138 us (56%)
  Pallas kernels  89.7 us (36%)
  local copies, waits for them, and re-layouts  9.16 us (4%)
  starting transfers between devices  8.27 us (3%)
    ppermute x3, waiting for transfers between devices, shards(): lax.ppermute(white, 'blk', [(i, (i + d) % blocks) for i in range(blocks)])  134 us
    pallas_call x1, Pallas kernels, correlate(): pl.pallas_call(correlate_kernel, grid=(CH // CBLK,), out_shape=jax.ShapeD...  76.5 us
    pallas_call x1, Pallas kernels, spectra(): pl.pallas_call(spectra_kernel, grid=(FRAMES // 2,), out_shape=(out, out),...  13.3 us
    unnamed x16, local copies, waits for them, and re-layouts  8.17 us
    ppermute x3, starting transfers between devices, shards(): lax.ppermute(white, 'blk', [(i, (i + d) % blocks) for i in range(blocks)])  6.35 us
  transfers between devices with their start and end apart: 4, of which 4 were waited for; matrix products, arithmetic and copies ran while one was open for 0% of the time, Pallas kernels for 0%

commit v1 on v0

--- a/solution.py
+++ b/solution.py
@@ -147,10 +147,108 @@
     )(jnp.asarray(main), jnp.asarray(tail), keep, record, record, record, record, halo)
 
 
+CHUNKS = 16
+SIZE = GROUPS // CHUNKS
+
+
+def exchange_kernel(own_ref, got_ref, send_sem, recv_sem):
+    me = lax.axis_index("blk")
+    count = lax.axis_size("blk")
+    ahead = lax.rem(me + 2, count)
+    behind = lax.rem(me + count - 2, count)
+    parity = lax.rem(me, 2)
+    beside = me + 1 - 2 * parity
+    barrier = pltpu.get_barrier_semaphore()
+    for other in (ahead, behind, beside):
+        pl.semaphore_signal(barrier, inc=1, device_id={"blk": other}, device_id_type=pl.DeviceIdType.MESH)
+    pl.semaphore_wait(barrier, 3)
+
+    def copy(source, which, target, slot, device):
+        rows = pl.ds(which * SIZE, SIZE)
+        src = own_ref.at[rows] if source == 0 else got_ref.at[source - 1, rows]
+        return pltpu.make_async_remote_copy(
+            src_ref=src,
+            dst_ref=got_ref.at[target - 1, rows],
+            send_sem=send_sem.at[slot, which],
+            recv_sem=recv_sem.at[target - 1, which],
+            device_id={"blk": device},
+            device_id_type=pl.DeviceIdType.MESH,
+        )
+
+    def arrived(source, which):
+        copy(0, which, source, 0, beside).wait_recv()
+
+    half = CHUNKS // 2
+    order = list(range(half, CHUNKS)) + list(range(half))
+
+    @pl.when(parity == 0)
+    def _():
+        sent = []
+
+        def send(*what):
+            sent.append(copy(*what))
+            sent[-1].start()
+
+        for i in range(CHUNKS):
+            send(0, order[i], 1, 0, beside)
+            if i < half:
+                send(0, i, 2, 1, ahead)
+        for i in range(CHUNKS):
+            arrived(1, i)
+            send(1, i, 3, 2, ahead)
+            if i < half:
+                arrived(2, i)
+                send(2, i, 3, 3, beside)
+        for i in range(half, CHUNKS):
+            arrived(2, i)
+        for i in range(CHUNKS):
+            arrived(3, i)
+        for item in sent:
+            item.wait_send()
+
+    @pl.when(parity == 1)
+    def _():
+        sent = []
+
+        def send(*what):
+            sent.append(copy(*what))
+            sent[-1].start()
+
+        for i in range(CHUNKS):
+            send(0, i, 2, 0, ahead)
+        for i in range(CHUNKS):
+            arrived(2, i)
+            send(2, i, 1, 1, beside)
+            if i < half:
+                arrived(1, order[i])
+                send(1, order[i], 3, 2, ahead)
+        for i in range(half, CHUNKS):
+            arrived(3, i)
+            send(3, i, 2, 3, beside)
+        for i in range(half):
+            arrived(1, i)
+        for i in range(half):
+            arrived(3, i)
+        for item in sent:
+            item.wait_send()
+
+
+def exchange(white):
+    return pl.pallas_call(
+        exchange_kernel,
+        out_shape=jax.ShapeDtypeStruct((3,) + white.shape, white.dtype),
+        in_specs=[pl.BlockSpec(memory_space=pl.ANY)],
+        out_specs=pl.BlockSpec(memory_space=pl.ANY),
+        scratch_shapes=[pltpu.SemaphoreType.DMA((4, CHUNKS)), pltpu.SemaphoreType.DMA((3, CHUNKS))],
+        compiler_params=pltpu.CompilerParams(collective_id=0, has_side_effects=True),
+        name="exchange",
+    )(white)
+
+
 CBLK = 32
 
 
-def correlate_kernel(spread_ref, lag_ref, white_ref, turned_ref, p1_ref, p2_ref, p3_ref, out_ref, cross):
+def correlate_kernel(spread_ref, lag_ref, white_ref, turned_ref, got_ref, out_ref, cross):
     rows = lax.broadcasted_iota(jnp.int32, (CBLK * 8, 256), 0)
     cols = lax.broadcasted_iota(jnp.int32, (CBLK * 8, 256), 1)
     diagonal = (rows % 4) == (cols % 4)
@@ -159,7 +257,7 @@
         own = jnp.concatenate([white_ref[group], turned_ref[group]], 1)
         left = lax.dot_general(spread_ref[...], own, NT, preferred_element_type=F32)
         left = jnp.where(diagonal, left, 0.0).astype(BF)
-        right = jnp.concatenate([white_ref[group], p1_ref[group], p2_ref[group], p3_ref[group]], 1)
+        right = jnp.concatenate([white_ref[group]] + [got_ref[d, group] for d in range(3)], 1)
         return jnp.dot(left, right, preferred_element_type=F32).reshape(CBLK, 8, 4 * CH)
 
     @pl.loop(0, GROUPS // 2)
@@ -175,30 +273,26 @@
             flat[pl.ds(c, NLAG, stride=CBLK), :] = result[:, d * CH : (d + 1) * CH]
 
 
-def correlate(white, turned, partners):
+def correlate(white, turned, got):
     whole = lambda *shape: pl.BlockSpec(shape, lambda i: (0,) * len(shape))
     spectrum = whole(GROUPS, 256, CH)
     return pl.pallas_call(
         correlate_kernel,
         grid=(CH // CBLK,),
         out_shape=jax.ShapeDtypeStruct((4, NLAG, CH, CH), F32),
-        in_specs=[pl.BlockSpec((CBLK * 8, 256), lambda i: (i, 0)), whole(NLAG, 256)] + [spectrum] * 5,
+        in_specs=[pl.BlockSpec((CBLK * 8, 256), lambda i: (i, 0)), whole(NLAG, 256)] + [spectrum] * 2 + [whole(3, GROUPS, 256, CH)],
         out_specs=pl.BlockSpec((4, NLAG, CBLK, CH), lambda i: (0, 0, i, 0)),
         scratch_shapes=[pltpu.VMEM((CBLK, 256, 4 * CH), BF)],
         compiler_params=pltpu.CompilerParams(vmem_limit_bytes=60 * 2**20),
         name="correlate",
-    )(jnp.asarray(spread_table()), jnp.asarray(lag_table()), white, turned, *partners)
+    )(jnp.asarray(spread_table()), jnp.asarray(lag_table()), white, turned, got)
 
 
 def shards(record, quality):
     count = lax.axis_size("pre")
     halo = lax.ppermute(record[:, :HALO], "pre", [(i, i - 1) for i in range(1, count)])
     white, turned = spectra(record, halo, quality)
-    blocks = lax.axis_size("blk")
-    partners = [
-        lax.ppermute(white, "blk", [(i, (i + d) % blocks) for i in range(blocks)]) for d in range(1, 4)
-    ]
-    return correlate(white, turned, partners)[None]
+    return correlate(white, turned, exchange(white))[None]
 
 
 def solution(mesh):

time: 247 us -> 186 us (0.75)
  waiting for transfers between devices: 138 us -> 3.56 us
  Pallas kernels: 89.7 us -> 169 us
  starting transfers between devices: 8.27 us -> 1.92 us
    ppermute x3 -> x0, waiting for transfers between devices: 134 us -> none  [shards(): lax.ppermute(white, 'blk', [(i, (i + d) % blocks) for i in range(blocks)])]
    pallas_call x0 -> x1, Pallas kernels: none -> 79.5 us  [exchange(): pl.pallas_call(exchange_kernel, out_shape=jax.ShapeDtypeStruct((3,) + whi...]
    ppermute x3 -> x0, starting transfers between devices: 6.35 us -> none  [shards(): lax.ppermute(white, 'blk', [(i, (i + d) % blocks) for i in range(blocks)])]
    unnamed x16 -> x10, local copies, waits for them, and re-layouts: 8.17 us -> 8.23 us
  transfers between devices with their start and end apart: 4 -> 1, of which waited for: 4 -> 1; matrix products, arithmetic and copies ran while one was open for 0% -> 0% of each run, Pallas kernels for 0% -> 0%
where the time goes in v1:
time: 186 us; the launch traced here: 185 us
  Pallas kernels  169 us (91%)
  local copies, waits for them, and re-layouts  9.21 us (5%)
  waiting for transfers between devices  3.56 us (2%)
  starting transfers between devices  1.92 us (1%)
    pallas_call x1, Pallas kernels, exchange(): pl.pallas_call(exchange_kernel, out_shape=jax.ShapeDtypeStruct((3,) + whi...  79.5 us
    pallas_call x1, Pallas kernels, correlate(): pl.pallas_call(correlate_kernel, grid=(CH // CBLK,), out_shape=jax.ShapeD...  76.6 us
    pallas_call x1, Pallas kernels, spectra(): pl.pallas_call(spectra_kernel, grid=(FRAMES // 2,), out_shape=(out, out),...  13.3 us
    unnamed x10, local copies, waits for them, and re-layouts  8.23 us
  transfers between devices with their start and end apart: 1, of which 1 were waited for; matrix products, arithmetic and copies ran while one was open for 0% of the time, Pallas kernels for 0%

profile of v1, /device:TPU:16, one launch (start us, length us, event | category | flops | bytes accessed | tf_op | source)
XLA Modules:
  0.0 184.7 jit_solution(74940313391537308)
XLA Ops:
  0.0 1.0 slice.3
  1.0 1.9 %collective-permute-start = (bf16[128,1152]{1,0:T(8,128)(2,1)S(1)}, bf16[128,1152]{1,0:T(8,128)(2,1)S(1)}, u32[]{:S(2)}, u32[]{:S(2)}) collective-permute-start(bf16[128,1152]{1,0:T(8,128)(2,1)S(1)} %slice.3), channel_id=1, source_target_pairs={{1,0},{2,1},{3,2},{5,4},{6,5},{7,6},{9,8},{10,9},{11,10},{13,12},{... | collective-permute-start | bytes 884744 | tf_op jit(solution)/shard_map/ppermute | solution.py:293
  2.9 0.7 convert_bitcast_fusion.quality_ref
  3.6 3.6 %collective-permute-done.halo_ref = bf16[128,1152]{1,0:T(8,128)(2,1)S(1)} collective-permute-done((bf16[128,1152]{1,0:T(8,128)(2,1)S(1)}, bf16[128,1152]{1,0:T(8,128)(2,1)S(1)}, u32[]{:S(2)}, u32[]{:S(2)}) %collective-permute-start) | collective-permute-done | bytes 294944 | tf_op jit(solution)/shard_map/ppermute | solution.py:293
  7.1 0.0 copy-start
  7.1 3.4 %copy-done = bf16[128,32768]{1,0:T(8,128)(2,1)S(1)} copy-done((bf16[128,32768]{1,0:T(8,128)(2,1)S(1)}, bf16[128,32768]{1,0:T(8,128)(2,1)}, u32[]{:S(2)}) %copy-start) | copy-done | bytes 8388632
  10.5 0.0 copy-start.3
  10.5 1.2 copy-done.3
  11.8 0.0 copy-start.4
  11.8 0.9 copy-done.4
  12.7 13.3 %spectra.1 = (bf16[32,256,128]{2,1,0:T(8,128)(2,1)S(1)}, bf16[32,256,128]{2,1,0:T(8,128)(2,1)S(1)}) custom-call(bf16[544,1024]{1,0:T(8,128)(2,1)S(1)} %copy-done.3, bf16[272,256]{1,0:T(8,128)(2,1)S(1)} %copy-done.4, f32[1,128]{1,0:T(1,128)S(1)} %convert_bitcast_fusion.quality_ref, bf16[128,32768]{1,0:T(8,128)(2,1)S(1)} %copy-done, ...), custom_call_target="tpu_custom_call" | custom-call | tf_op jit(solution)/shard_map/spectra/pallas_call | solution.py:129
  26.0 0.0 copy-start.1
  26.0 1.3 copy-done.1
  27.3 0.0 copy-start.2
  27.3 1.4 copy-done.2
  28.7 79.5 %exchange.1.got_ref = bf16[3,32,256,128]{3,2,1,0:T(8,128)(2,1)} custom-call(bf16[32,256,128]{2,1,0:T(8,128)(2,1)} %copy-done.1), custom_call_target="tpu_custom_call" | custom-call | tf_op jit(solution)/shard_map/exchange/pallas_call | solution.py:237
  108.1 76.6 %correlate.1 = f32[4,64,128,128]{3,2,1,0:T(8,128)} custom-call(bf16[1024,256]{1,0:T(8,128)(2,1)} %constant.10.clone.spread_ref, bf16[64,256]{1,0:T(8,128)(2,1)} %constant.11.clone.lag_ref, bf16[32,256,128]{2,1,0:T(8,128)(2,1)} %copy-done.1, bf16[32,256,128]{2,1,0:T(8,128)(2,1)} %copy-done.2, bf16[3,32,256,128]{3,2,1,0:T(8,128)(2,1)} %exchange.1.got_ref), custom_call_target="tpu_custom_call" | custom-call | tf_op jit(solution)/shard_map/correlate/pallas_call | solution.py:279
Async XLA Ops:
  1.0 6.1 %collective-permute-start = (bf16[128,1152]{1,0:T(8,128)(2,1)S(1)}, bf16[128,1152]{1,0:T(8,128)(2,1)S(1)}, u32[]{:S(2)}, u32[]{:S(2)}) collective-permute-start(bf16[128,1152]{1,0:T(8,128)(2,1)S(1)} %slice.3), channel_id=1, source_target_pairs={{1,0},{2,1},{3,2},{5,4},{6,5},{7,6},{9,8},{10,9},{11,10},{13,12},{... | collective-permute-start | bytes 884744 | tf_op jit(solution)/shard_map/ppermute | solution.py:293
  7.1 3.4 %copy-start = (bf16[128,32768]{1,0:T(8,128)(2,1)S(1)}, bf16[128,32768]{1,0:T(8,128)(2,1)}, u32[]{:S(2)}) copy-start(bf16[128,32768]{1,0:T(8,128)(2,1)} %three_ref.1) | copy-start | bytes 25165828
  10.5 1.2 copy-start.3
  11.8 0.9 copy-start.4
  26.0 1.3 copy-start.1
  27.3 1.4 copy-start.2

commit v2 on v0

--- a/solution.py
+++ b/solution.py
@@ -142,63 +142,242 @@
         ],
         out_specs=[pl.BlockSpec((GROUPS, 16, CH), lambda i: (0, i, 0))] * 2,
         scratch_shapes=[pltpu.VMEM((GROUPS + 2, 8, CH), F32)],
-        compiler_params=pltpu.CompilerParams(vmem_limit_bytes=40 * 2**20),
+        compiler_params=pltpu.CompilerParams(vmem_limit_bytes=60 * 2**20),
         name="spectra",
     )(jnp.asarray(main), jnp.asarray(tail), keep, record, record, record, record, halo)
 
 
-CBLK = 32
-
-
-def correlate_kernel(spread_ref, lag_ref, white_ref, turned_ref, p1_ref, p2_ref, p3_ref, out_ref, cross):
-    rows = lax.broadcasted_iota(jnp.int32, (CBLK * 8, 256), 0)
-    cols = lax.broadcasted_iota(jnp.int32, (CBLK * 8, 256), 1)
+CHUNKS = GROUPS // 2
+PART = 32
+
+
+def exchange_kernel(spread_ref, lag_ref, white_ref, turned_ref, near_ref, far_ref,
+                    got, left, cross, fars, nears, send_sem, recv_sem, far_sem, near_sem):
+    me = lax.axis_index("blk")
+    count = lax.axis_size("blk")
+    ahead = lax.rem(me + 2, count)
+    behind = lax.rem(me + count - 2, count)
+    parity = lax.rem(me, 2)
+    beside = me + 1 - 2 * parity
+    barrier = pltpu.get_barrier_semaphore()
+    for other in (ahead, behind, beside):
+        pl.semaphore_signal(barrier, inc=1, device_id={"blk": other}, device_id_type=pl.DeviceIdType.MESH)
+    pl.semaphore_wait(barrier, 3)
+
+    def copy(source, which, target, slot, device):
+        rows = pl.ds(which * 2, 2)
+        src = white_ref.at[rows] if source == 0 else got.at[source - 1, rows]
+        return pltpu.make_async_remote_copy(
+            src_ref=src,
+            dst_ref=got.at[target - 1, rows],
+            send_sem=send_sem.at[slot, which],
+            recv_sem=recv_sem.at[target - 1, which],
+            device_id={"blk": device},
+            device_id_type=pl.DeviceIdType.MESH,
+        )
+
+    def arrived(source, which):
+        copy(0, which, source, 0, beside).wait_recv()
+
+    @pl.when(parity == 0)
+    def _():
+        for i in range(CHUNKS):
+            copy(0, i, 1, 0, beside).start()
+            if i % 2 == 0:
+                copy(0, i, 2, 1, ahead).start()
+
+    @pl.when(parity == 1)
+    def _():
+        for i in range(CHUNKS):
+            copy(0, i, 2, 0, ahead).start()
+
+    rows = lax.broadcasted_iota(jnp.int32, (PART * 8, 256), 0)
+    cols = lax.broadcasted_iota(jnp.int32, (PART * 8, 256), 1)
     diagonal = (rows % 4) == (cols % 4)
 
-    def stage(group):
-        own = jnp.concatenate([white_ref[group], turned_ref[group]], 1)
-        left = lax.dot_general(spread_ref[...], own, NT, preferred_element_type=F32)
-        left = jnp.where(diagonal, left, 0.0).astype(BF)
-        right = jnp.concatenate([white_ref[group], p1_ref[group], p2_ref[group], p3_ref[group]], 1)
-        return jnp.dot(left, right, preferred_element_type=F32).reshape(CBLK, 8, 4 * CH)
-
-    @pl.loop(0, GROUPS // 2)
-    def _(pair):
-        both = jnp.concatenate([stage(2 * pair), stage(2 * pair + 1)], 1)
-        cross[:, pl.ds(pl.multiple_of(pair * 16, 16), 16), :] = both.astype(BF)
-
-    @pl.loop(0, CBLK)
-    def _(c):
-        result = jnp.dot(lag_ref[...], cross[c], preferred_element_type=F32)
-        for d in range(4):
-            flat = out_ref.at[d].reshape(NLAG * CBLK, CH)
-            flat[pl.ds(c, NLAG, stride=CBLK), :] = result[:, d * CH : (d + 1) * CH]
-
-
-def correlate(white, turned, partners):
-    whole = lambda *shape: pl.BlockSpec(shape, lambda i: (0,) * len(shape))
-    spectrum = whole(GROUPS, 256, CH)
+    @pl.loop(0, CHUNKS)
+    def _(p):
+        even = lax.rem(p, 2) == 0
+
+        @pl.when(parity == 0)
+        def _():
+            arrived(1, p)
+            copy(1, p, 3, 2, ahead).start()
+
+            @pl.when(even)
+            def _():
+                arrived(2, p)
+                copy(2, p, 3, 3, beside).start()
+
+        @pl.when(parity == 1)
+        def _():
+            arrived(2, p)
+            copy(2, p, 1, 1, beside).start()
+            arrived(1, p)
+
+            @pl.when(jnp.logical_not(even))
+            def _():
+                copy(1, p, 3, 2, ahead).start()
+
+        for part in range(CH // PART):
+            lines = pl.ds(part * PART * 8, PART * 8)
+            pieces = []
+            for j in range(2):
+                group = 2 * p + j
+                own = jnp.concatenate([white_ref[group], turned_ref[group]], 1)
+                table = lax.dot_general(spread_ref[lines, :], own, NT, preferred_element_type=F32)
+                table = jnp.where(diagonal, table, 0.0).astype(BF)
+                left[group, lines, :] = table
+                right = jnp.concatenate([white_ref[group], got[0, group]], 1)
+                pieces.append(jnp.dot(table, right, preferred_element_type=F32).reshape(PART, 8, 2 * CH))
+            both = jnp.concatenate(pieces, 1).astype(BF)
+            cross[pl.ds(part * PART, PART), pl.ds(pl.multiple_of(p * 16, 16), 16), :] = both
+
+    def store_far(p):
+        at = pl.ds(pl.multiple_of(p * 16, 16), 16)
+        return pltpu.make_async_copy(fars.at[lax.rem(p, 2)], far_ref.at[:, at, :], far_sem.at[lax.rem(p, 2)])
+
+    def store_near(p):
+        at = pl.ds(pl.multiple_of(p * 8, 8), 8)
+        return pltpu.make_async_copy(nears.at[lax.rem(p, 2)], near_ref.at[:, :, at, :], near_sem.at[lax.rem(p, 2)])
+
+    @pl.loop(0, CHUNKS)
+    def _(p):
+        even = lax.rem(p, 2) == 0
+        buffer = lax.rem(p, 2)
+
+        @pl.when(parity == 0)
+        def _():
+            arrived(3, p)
+
+            @pl.when(jnp.logical_not(even))
+            def _():
+                arrived(2, p)
+
+        @pl.when(parity == 1)
+        def _():
+            arrived(3, p)
+
+            @pl.when(jnp.logical_not(even))
+            def _():
+                copy(3, p, 2, 3, beside).start()
+
+        @pl.when(p >= 2)
+        def _():
+            store_far(p - 2).wait()
+            store_near(p - 2).wait()
+
+        for part in range(CH // PART):
+            lines = pl.ds(part * PART * 8, PART * 8)
+            pieces = []
+            for j in range(2):
+                group = 2 * p + j
+                right = jnp.concatenate([got[1, group], got[2, group]], 1)
+                pieces.append(
+                    jnp.dot(left[group, lines, :], right, preferred_element_type=F32).reshape(PART, 8, 2 * CH))
+            fars[buffer, pl.ds(part * PART, PART)] = jnp.concatenate(pieces, 1).astype(BF)
+        store_far(p).start()
+
+        for j in range(8):
+            result = jnp.dot(lag_ref[...], cross[p * 8 + j], preferred_element_type=F32)
+            for d in range(2):
+                flat = nears.at[buffer, d].reshape(NLAG * 8, CH)
+                flat[pl.ds(j, NLAG, stride=8), :] = result[:, d * CH : (d + 1) * CH]
+        store_near(p).start()
+
+    for p in (CHUNKS - 2, CHUNKS - 1):
+        store_far(p).wait()
+        store_near(p).wait()
+
+    @pl.loop(0, CHUNKS)
+    def _(p):
+        even = lax.rem(p, 2) == 0
+
+        @pl.when(parity == 0)
+        def _():
+            copy(0, p, 1, 0, beside).wait_send()
+            copy(1, p, 3, 2, ahead).wait_send()
+
+            @pl.when(even)
+            def _():
+                copy(0, p, 2, 1, ahead).wait_send()
+                copy(2, p, 3, 3, beside).wait_send()
+
+        @pl.when(parity == 1)
+        def _():
+            copy(0, p, 2, 0, ahead).wait_send()
+            copy(2, p, 1, 1, beside).wait_send()
+
+            @pl.when(jnp.logical_not(even))
+            def _():
+                copy(1, p, 3, 2, ahead).wait_send()
+                copy(3, p, 2, 3, beside).wait_send()
+
+
+def exchange(white, turned):
+    inside = pl.BlockSpec(memory_space=pltpu.VMEM)
     return pl.pallas_call(
-        correlate_kernel,
-        grid=(CH // CBLK,),
+        exchange_kernel,
+        out_shape=(
+            jax.ShapeDtypeStruct((2, NLAG, CH, CH), F32),
+            jax.ShapeDtypeStruct((CH, 2 * FB, 2 * CH), BF),
+        ),
+        in_specs=[inside] * 4,
+        out_specs=(pl.BlockSpec(memory_space=pl.ANY),) * 2,
+        scratch_shapes=[
+            pltpu.VMEM((3, GROUPS, 256, CH), BF),
+            pltpu.VMEM((GROUPS, CH * 8, 256), BF),
+            pltpu.VMEM((CH, 2 * FB, 2 * CH), BF),
+            pltpu.VMEM((2, CH, 16, 2 * CH), BF),
+            pltpu.VMEM((2, 2, NLAG, 8, CH), F32),
+            pltpu.SemaphoreType.DMA((4, CHUNKS)),
+            pltpu.SemaphoreType.DMA((3, CHUNKS)),
+            pltpu.SemaphoreType.DMA((2,)),
+            pltpu.SemaphoreType.DMA((2,)),
+        ],
+        compiler_params=pltpu.CompilerParams(
+            collective_id=0, has_side_effects=True, vmem_limit_bytes=60 * 2**20),
+        name="exchange",
+    )(jnp.asarray(spread_table()), jnp.asarray(lag_table()), white, turned)
+
+
+LAST = 16
+
+
+def last_kernel(lag_ref, near_ref, far_ref, out_ref):
+    out_ref[0:2] = near_ref[...]
+
+    @pl.loop(0, LAST // 8)
+    def _(step):
+        for j in range(8):
+            c = step * 8 + j
+            result = jnp.dot(lag_ref[...], far_ref[c], preferred_element_type=F32)
+            for d in range(2):
+                flat = out_ref.at[2 + d].reshape(NLAG * LAST, CH)
+                flat[pl.ds(c, NLAG, stride=LAST), :] = result[:, d * CH : (d + 1) * CH]
+
+
+def last(near, far):
+    return pl.pallas_call(
+        last_kernel,
+        grid=(CH // LAST,),
         out_shape=jax.ShapeDtypeStruct((4, NLAG, CH, CH), F32),
-        in_specs=[pl.BlockSpec((CBLK * 8, 256), lambda i: (i, 0)), whole(NLAG, 256)] + [spectrum] * 5,
-        out_specs=pl.BlockSpec((4, NLAG, CBLK, CH), lambda i: (0, 0, i, 0)),
-        scratch_shapes=[pltpu.VMEM((CBLK, 256, 4 * CH), BF)],
+        in_specs=[
+            pl.BlockSpec((NLAG, 2 * FB), lambda i: (0, 0)),
+            pl.BlockSpec((2, NLAG, LAST, CH), lambda i: (0, 0, i, 0)),
+            pl.BlockSpec((LAST, 2 * FB, 2 * CH), lambda i: (i, 0, 0)),
+        ],
+        out_specs=pl.BlockSpec((4, NLAG, LAST, CH), lambda i: (0, 0, i, 0)),
         compiler_params=pltpu.CompilerParams(vmem_limit_bytes=60 * 2**20),
-        name="correlate",
-    )(jnp.asarray(spread_table()), jnp.asarray(lag_table()), white, turned, *partners)
+        name="last",
+    )(jnp.asarray(lag_table()), near, far)
 
 
 def shards(record, quality):
     count = lax.axis_size("pre")
     halo = lax.ppermute(record[:, :HALO], "pre", [(i, i - 1) for i in range(1, count)])
     white, turned = spectra(record, halo, quality)
-    blocks = lax.axis_size("blk")
-    partners = [
-        lax.ppermute(white, "blk", [(i, (i + d) % blocks) for i in range(blocks)]) for d in range(1, 4)
-    ]
-    return correlate(white, turned, partners)[None]
+    return last(*exchange(white, turned))[None]
 
 
 def solution(mesh):

time: 247 us -> 129 us (0.52)
  waiting for transfers between devices: 138 us -> 3.04 us
  Pallas kernels: 89.7 us -> 119 us
  local copies, waits for them, and re-layouts: 9.16 us -> 1.69 us
  starting transfers between devices: 8.27 us -> 1.92 us
    ppermute x3 -> x0, waiting for transfers between devices: 134 us -> none  [shards(): lax.ppermute(white, 'blk', [(i, (i + d) % blocks) for i in range(blocks)])]
    pallas_call x1 -> x2, Pallas kernels: 76.5 us -> 102 us  [the longest x1 84 us: exchange(): pl.pallas_call(exchange_kernel, out_shape=(jax.ShapeDtypeStruct((2, NLAG,...]
    unnamed x16 -> x2, local copies, waits for them, and re-layouts: 8.17 us -> 0.71 us
    ppermute x3 -> x0, starting transfers between devices: 6.35 us -> none  [shards(): lax.ppermute(white, 'blk', [(i, (i + d) % blocks) for i in range(blocks)])]
    pallas_call x1, Pallas kernels: 13.3 us -> 17.4 us  [spectra(): pl.pallas_call(spectra_kernel, grid=(FRAMES // 2,), out_shape=(out, out),...]
  transfers between devices with their start and end apart: 4 -> 1, of which waited for: 4 -> 1; matrix products, arithmetic and copies ran while one was open for 0% -> 1% of each run, Pallas kernels for 0% -> 0%
where the time goes in v2:
time: 129 us; the launch traced here: 127 us
  Pallas kernels  119 us (92%)
  waiting for transfers between devices  3.04 us (2%)
  starting transfers between devices  1.92 us (1%)
  local copies, waits for them, and re-layouts  1.69 us (1%)
    pallas_call x1, Pallas kernels, exchange(): pl.pallas_call(exchange_kernel, out_shape=(jax.ShapeDtypeStruct((2, NLAG,...  84 us
    pallas_call x1, Pallas kernels, last(): pl.pallas_call(last_kernel, grid=(CH // LAST,), out_shape=jax.ShapeDtypeS...  18 us
    pallas_call x1, Pallas kernels, spectra(): pl.pallas_call(spectra_kernel, grid=(FRAMES // 2,), out_shape=(out, out),...  17.4 us
    ppermute x1, waiting for transfers between devices, shards(): lax.ppermute(record[:, :HALO], 'pre', [(i, i - 1) for i in range(1, count)])  3.04 us
  transfers between devices with their start and end apart: 1, of which 1 were waited for; matrix products, arithmetic and copies ran while one was open for 1% of the time, Pallas kernels for 0%

profile of v2, /device:TPU:16, one launch (start us, length us, event | category | flops | bytes accessed | tf_op | source)
XLA Modules:
  0.0 127.2 jit_solution(646489909711990444)
XLA Ops:
  0.0 1.0 slice.3
  1.0 1.9 %collective-permute-start = (bf16[128,1152]{1,0:T(8,128)(2,1)S(1)}, bf16[128,1152]{1,0:T(8,128)(2,1)S(1)}, u32[]{:S(2)}, u32[]{:S(2)}) collective-permute-start(bf16[128,1152]{1,0:T(8,128)(2,1)S(1)} %slice.3), channel_id=1, source_target_pairs={{1,0},{2,1},{3,2},{5,4},{6,5},{7,6},{9,8},{10,9},{11,10},{13,12},{... | collective-permute-start | bytes 884744 | tf_op jit(solution)/shard_map/ppermute | solution.py:378
  2.9 1.2 convert_bitcast_fusion.quality_ref
  4.1 3.0 %collective-permute-done.halo_ref = bf16[128,1152]{1,0:T(8,128)(2,1)S(1)} collective-permute-done((bf16[128,1152]{1,0:T(8,128)(2,1)S(1)}, bf16[128,1152]{1,0:T(8,128)(2,1)S(1)}, u32[]{:S(2)}, u32[]{:S(2)}) %collective-permute-start) | collective-permute-done | bytes 294944 | tf_op jit(solution)/shard_map/ppermute | solution.py:378
  7.1 0.0 copy-start
  7.1 0.7 copy-done
  7.8 17.4 %spectra.1 = (bf16[32,256,128]{2,1,0:T(8,128)(2,1)}, bf16[32,256,128]{2,1,0:T(8,128)(2,1)}) custom-call(bf16[544,1024]{1,0:T(8,128)(2,1)} %constant.8.clone.main_ref, bf16[272,256]{1,0:T(8,128)(2,1)} %constant.9.clone.tail_ref, f32[1,128]{1,0:T(1,128)} %convert_bitcast_fusion.quality_ref, bf16[128,32768]{1,0:T(8,128)(2,1)} %three_ref.1, ...), custom_call_target="tpu_custom_call" | custom-call | tf_op jit(solution)/shard_map/spectra/pallas_call | solution.py:129
  25.2 84.0 %exchange.1 = (f32[2,64,128,128]{3,2,1,0:T(8,128)}, bf16[128,256,256]{2,1,0:T(8,128)(2,1)}) custom-call(bf16[1024,256]{1,0:T(8,128)(2,1)} %constant.10.clone.spread_ref, bf16[64,256]{1,0:T(8,128)(2,1)} %constant.11.clone.lag_ref, bf16[32,256,128]{2,1,0:T(8,128)(2,1)} %get-tuple-element.9.white_ref, bf16[32,256,128]{2,1,0:T(8,128)(2,1)} %get-tuple-element.10.turned_ref), custom_call_target="tpu_custom_call" | custom-call | tf_op jit(solution)/shard_map/exchange/pallas_call | solution.py:319
  109.3 18.0 %last.1 = f32[4,64,128,128]{3,2,1,0:T(8,128)} custom-call(bf16[64,256]{1,0:T(8,128)(2,1)} %constant.11.clone.lag_ref, f32[2,64,128,128]{3,2,1,0:T(8,128)} %get-tuple-element.11.near_ref, bf16[128,256,256]{2,1,0:T(8,128)(2,1)} %get-tuple-element.12.far_ref), custom_call_target="tpu_custom_call" | custom-call | tf_op jit(solution)/shard_map/last/pallas_call | solution.py:361
Async XLA Ops:
  1.0 6.1 %collective-permute-start = (bf16[128,1152]{1,0:T(8,128)(2,1)S(1)}, bf16[128,1152]{1,0:T(8,128)(2,1)S(1)}, u32[]{:S(2)}, u32[]{:S(2)}) collective-permute-start(bf16[128,1152]{1,0:T(8,128)(2,1)S(1)} %slice.3), channel_id=1, source_target_pairs={{1,0},{2,1},{3,2},{5,4},{6,5},{7,6},{9,8},{10,9},{11,10},{13,12},{... | collective-permute-start | bytes 884744 | tf_op jit(solution)/shard_map/ppermute | solution.py:378
  7.1 0.7 copy-start

commit v3 on v0

v3 whole, which is shorter than its diff:
```python
import math

import jax
import jax.numpy as jnp
import ml_dtypes
import numpy as np
from jax import lax
from jax.experimental import pallas as pl
from jax.experimental.pallas import tpu as pltpu
from jax.sharding import PartitionSpec as P

M = 512
R = 4
KT = 16
FB = 128
NLAG = 64
BAND0 = 16
CH = 128
HALF = 1024
FRAMES = 32
GROUPS = 32
ROWS = (GROUPS + 2) * 8
HALO = HALF + 128
NT = (((1,), (1,)), ((), ()))
BF = jnp.bfloat16
F32 = jnp.float32


def filter_taps():
    index = np.arange(KT, dtype=np.float32)
    centre = np.float32((KT - 1) / 2.0)
    shaped = np.sinc((index - centre) / np.float32(R)) * (
        0.54 - 0.46 * np.cos(2.0 * math.pi * index / (KT - 1))
    )
    return (shaped / np.sum(shaped)).astype(np.float32).astype(ml_dtypes.bfloat16)


def split(table):
    high = table.astype(np.float32).astype(ml_dtypes.bfloat16)
    low = (table - high.astype(np.float64)).astype(np.float32).astype(ml_dtypes.bfloat16)
    return high, low


def half_tables():
    taps = filter_taps().astype(np.float64)
    toeplitz = np.zeros((M // 2, HALF + 128))
    for m in range(M // 2):
        toeplitz[m, R * m : R * m + KT] = taps
    group = np.arange(-1, GROUPS + 1)
    bins = BAND0 + group[:, None] + 32 * np.arange(4)[None, :]
    phase = 2.0 * math.pi * ((bins[:, :, None] * np.arange(M // 2)) % M) / M
    both = np.stack([np.cos(phase), -np.sin(phase)], 1).reshape(ROWS, M // 2)
    table = both @ toeplitz
    high, low = split(table)
    main = np.concatenate([high[:, :HALF], low[:, :HALF]], 0)
    tail = np.concatenate([high[:, HALF:], low[:, HALF:]], 1)
    return main, tail


def lag_table():
    lags = np.arange(NLAG) - NLAG // 2
    bins = (BAND0 + np.arange(GROUPS)[:, None, None] + 32 * np.arange(4)[None, None, :])
    phase = 2.0 * math.pi * (((lags[:, None, None, None] + M) * bins[None]) % M) / M
    both = np.concatenate([np.cos(phase), -np.sin(phase)], 2).reshape(NLAG, 2 * FB)
    rounded = both.astype(np.float32).astype(ml_dtypes.bfloat16).astype(np.float32)
    return (rounded / 64.0).astype(ml_dtypes.bfloat16)


def spread_table():
    table = np.zeros((CH, 2, 4, 2, CH), np.float32)
    for c in range(CH):
        for o in range(2):
            table[c, o, :, o, c] = 1.0
    return table.reshape(CH * 8, 2 * CH).astype(ml_dtypes.bfloat16)


CHUNKS = 16
PART = 32
LENGTH = FRAMES * HALF


def exchange_kernel(record_ref, quality_ref, main_hbm, tail_hbm, spread_hbm, lag_hbm, near_ref, far_ref,
                    rec, main, tail, spread, lag, held, white, turned, got, left, cross, fars, nears,
                    send_sem, recv_sem, far_sem, near_sem, rec_sem, table_sem, halo_sem):
    tables = [
        pltpu.make_async_copy(source, target, table_sem.at[i])
        for i, (source, target) in enumerate(
            [(main_hbm, main), (tail_hbm, tail), (spread_hbm, spread), (lag_hbm, lag)])
    ]

    def piece(i):
        at = pl.ds(pl.multiple_of(i * 2 * HALF, 2 * HALF), 2 * HALF)
        return pltpu.make_async_copy(record_ref.at[:, at], rec.at[:, at], rec_sem.at[i])

    piece(0).start()
    tables[0].start()
    tables[1].start()
    for i in range(1, FRAMES // 2):
        piece(i).start()
    tables[2].start()
    tables[3].start()

    me = lax.axis_index("blk")
    count = lax.axis_size("blk")
    ahead = lax.rem(me + 2, count)
    behind = lax.rem(me + count - 2, count)
    parity = lax.rem(me, 2)
    beside = me + 1 - 2 * parity
    segment = lax.axis_index("pre")
    segments = lax.axis_size("pre")
    sooner = lax.rem(segment + segments - 1, segments)
    later = lax.rem(segment + 1, segments)
    barrier = pltpu.get_barrier_semaphore()
    for other in (ahead, behind, beside):
        pl.semaphore_signal(barrier, inc=1, device_id={"blk": other}, device_id_type=pl.DeviceIdType.MESH)
    for other in (sooner, later):
        pl.semaphore_signal(barrier, inc=1, device_id={"pre": other}, device_id_type=pl.DeviceIdType.MESH)
    pl.semaphore_wait(barrier, 5)

    halo = pltpu.make_async_remote_copy(
        src_ref=record_ref.at[:, pl.ds(0, HALO)],
        dst_ref=rec.at[:, pl.ds(LENGTH, HALO)],
        send_sem=halo_sem.at[0],
        recv_sem=halo_sem.at[1],
        device_id={"pre": sooner},
        device_id_type=pl.DeviceIdType.MESH,
    )

    @pl.when(segment > 0)
    def _():
        halo.start()

    @pl.when(segment == segments - 1)
    def _():
        rec[:, LENGTH:] = jnp.zeros((CH, HALO), BF)

    def view(ref, half, which):
        if half == 0:
            return ref.at[:, pl.ds(pl.multiple_of(which * 16, 16), 16), :]
        return ref.at[pl.ds(which * 4, 4), pl.ds(128, 128), :]

    def copy(half, which, source, target, slot, device):
        return pltpu.make_async_remote_copy(
            src_ref=view(white if source == 0 else got.at[source - 1], half, which),
            dst_ref=view(got.at[target - 1], half, which),
            send_sem=send_sem.at[slot, half * 8 + which],
            recv_sem=recv_sem.at[target - 1, half * 8 + which],
            device_id={"blk": device},
            device_id_type=pl.DeviceIdType.MESH,
        )

    def arrived(half, which, source):
        copy(half, which, 0, source, 0, beside).wait_recv()

    def on(condition):
        return lambda body: pl.when(condition)(body)

    def offer(half, which):
        @on(parity == 0)
        def _():
            copy(half, which, 0, 1, 0, beside).start()

            @on(lax.rem(which, 2) == 0)
            def _():
                copy(half, which, 0, 2, 1, ahead).start()

        @on(parity == 1)
        def _():
            copy(half, which, 0, 2, 0, ahead).start()

    def relay(half, which):
        @on(parity == 0)
        def _():
            arrived(half, which, 1)
            copy(half, which, 1, 3, 2, ahead).start()

            @on(lax.rem(which, 2) == 0)
            def _():
                arrived(half, which, 2)
                copy(half, which, 2, 3, 3, beside).start()

        @on(parity == 1)
        def _():
            arrived(half, which, 2)
            copy(half, which, 2, 1, 1, beside).start()
            arrived(half, which, 1)

            @on(lax.rem(which, 2) == 1)
            def _():
                copy(half, which, 1, 3, 2, ahead).start()

    def finish(half, which):
        arrived(half, which, 3)

        @on(lax.rem(which, 2) == 1)
        def _():
            @on(parity == 0)
            def _():
                arrived(half, which, 2)

            @on(parity == 1)
            def _():
                copy(half, which, 3, 2, 3, beside).start()

    def transform(raw, after):
        both = lax.dot_general(main[...], raw, NT, preferred_element_type=F32)
        ends = jnp.concatenate([after, after], 1)
        return (both[:ROWS] + both[ROWS:]) + lax.dot_general(
            tail[...], ends, NT, preferred_element_type=F32)

    piece(0).wait()
    tables[0].wait()
    tables[1].wait()
    held[...] = transform(rec[:, :HALF], rec[:, HALF : HALF + 128]).reshape(GROUPS + 2, 8, CH)
    keep = quality_ref[...].astype(F32).reshape(1, 1, CH)

    def frames(step):
        start = pl.multiple_of(step * 2 * HALF + HALF, HALF)
        one = pl.ds(start, HALF)
        two = pl.ds(pl.multiple_of(start + HALF, HALF), HALF)
        raw = jnp.concatenate([rec[:, one], rec[:, two]], 0)
        after = jnp.concatenate([
            rec[:, pl.ds(pl.multiple_of(start + HALF, HALF), 128)],
            rec[:, pl.ds(pl.multiple_of(start + 2 * HALF, HALF), 128)]], 0)
        pair = transform(raw, after)
        zero = held[...]
        first = pair[:, :CH].reshape(GROUPS + 2, 8, CH)
        second = pair[:, CH:].reshape(GROUPS + 2, 8, CH)
        held[...] = second
        group = lax.broadcasted_iota(jnp.int32, (GROUPS, 8, CH), 0)
        odd = (group % 2) == 1
        row = lax.broadcasted_iota(jnp.int32, (GROUPS, 8, CH), 1)

        def whiten(front, back):
            side = 0.25 * (front[:GROUPS] + front[2:])
            spec = 0.5 * front[1 : GROUPS + 1] - side
            other = 0.5 * back[1 : GROUPS + 1] + 0.25 * (back[:GROUPS] + back[2:])
            spec = spec + jnp.where(odd, -other, other)
            square = spec * spec
            level = jnp.sum(jnp.sum(square, 0), 0, keepdims=True).reshape(1, 1, CH) * (1.0 / FB)
            power = square + pltpu.roll(square, 4, 1)
            plain = spec * lax.rsqrt(power + (0.1 * level + 1e-06)) * keep
            swapped = pltpu.roll(plain, 4, 1)
            return plain, jnp.where(row < 4, swapped, -swapped)

        w0, t0 = whiten(zero, first)
        w1, t1 = whiten(first, second)
        at = pl.ds(pl.multiple_of(step * 16, 16), 16)
        white[:, at, :] = jnp.concatenate([w0, w1], 1).astype(BF)
        turned[:, at, :] = jnp.concatenate([t0, t1], 1).astype(BF)

    @pl.loop(0, 8)
    def _(step):
        piece(step + 1).wait()
        frames(step)
        offer(0, step)

    @pl.loop(8, FRAMES // 2)
    def _(step):
        @on(step < FRAMES // 2 - 1)
        def _():
            piece(step + 1).wait()

        @on(jnp.logical_and(step == FRAMES // 2 - 1, segment < segments - 1))
        def _():
            halo.wait_recv()

        frames(step)

        @on(lax.rem(step, 3) == 0)
        def _():
            relay(0, lax.div(step, 3) - 3)

    @pl.loop(0, 8)
    def _(which):
        offer(1, which)

    tables[2].wait()
    tables[3].wait()
    rows = lax.broadcasted_iota(jnp.int32, (PART * 8, 256), 0)
    cols = lax.broadcasted_iota(jnp.int32, (PART * 8, 256), 1)
    diagonal = (rows % 4) == (cols % 4)

    @pl.loop(3, 8)
    def _(which):
        relay(0, which)

        @on(which < 7)
        def _():
            @pl.loop(0, 8)
            def _(j):
                group = (which - 3) * 8 + j
                own = jnp.concatenate([white[group], turned[group]], 1)
                for part in range(CH // PART):
                    lines = pl.ds(part * PART * 8, PART * 8)
                    table = lax.dot_general(spread[lines, :], own, NT, preferred_element_type=F32)
                    left[group, lines, :] = jnp.where(diagonal, table, 0.0).astype(BF)

    def products(pair, one, two, store):
        for part in range(CH // PART):
            lines = pl.ds(part * PART * 8, PART * 8)
            pieces = []
            for j in range(2):
                group = 2 * pair + j
                right = jnp.concatenate([one[group], two[group]], 1)
                pieces.append(
                    jnp.dot(left[group, lines, :], right, preferred_element_type=F32).reshape(PART, 8, 2 * CH))
            store(part, jnp.concatenate(pieces, 1).astype(BF))

    @pl.loop(0, 8)
    def _(which):
        relay(1, which)

        @pl.loop(0, 2)
        def _(j):
            pair = which * 2 + j

            def store(part, value):
                cross[pl.ds(part * PART, PART), pl.ds(pl.multiple_of(pair * 16, 16), 16), :] = value

            products(pair, white, got.at[0], store)

    def store_far(which):
        at = pl.ds(pl.multiple_of(which * 32, 32), 32)
        buffer = lax.rem(which, 2)
        return pltpu.make_async_copy(fars.at[buffer], far_ref.at[:, at, :], far_sem.at[buffer])

    def store_near(which):
        at = pl.ds(pl.multiple_of(which * 8, 8), 8)
        buffer = lax.rem(which, 2)
        return pltpu.make_async_copy(nears.at[buffer], near_ref.at[:, :, at, :], near_sem.at[buffer])

    @pl.loop(0, 8)
    def _(which):
        finish(0, which)
        for buffer in range(2):
            step = which * 2 + buffer

            @on(which > 0)
            def _():
                store_near(step - 2).wait()

            for j in range(8):
                result = jnp.dot(lag[...], cross[step * 8 + j], preferred_element_type=F32)
                for d in range(2):
                    flat = nears.at[buffer, d].reshape(NLAG * 8, CH)
                    flat[pl.ds(j, NLAG, stride=8), :] = result[:, d * CH : (d + 1) * CH]
            store_near(step).start()

    @pl.loop(0, 8)
    def _(which):
        finish(1, which)

        @on(which > 1)
        def _():
            store_far(which - 2).wait()

        @pl.loop(0, 2)
        def _(j):
            def store(part, value):
                fars[lax.rem(which, 2), pl.ds(part * PART, PART),
                     pl.ds(pl.multiple_of(j * 16, 16), 16), :] = value

            products(which * 2 + j, got.at[1], got.at[2], store)

        store_far(which).start()

    for step in (CHUNKS - 2, CHUNKS - 1):
        store_near(step).wait()
    for which in (6, 7):
        store_far(which).wait()

    @on(segment > 0)
    def _():
        halo.wait_send()

    for half in range(2):
        @pl.loop(0, 8)
        def _(which):
            copy(half, which, 0, 1, 0, beside).wait_send()

            @on(parity == 0)
            def _():
                copy(half, which, 1, 3, 2, ahead).wait_send()

                @on(lax.rem(which, 2) == 0)
                def _():
                    copy(half, which, 0, 2, 1, ahead).wait_send()
                    copy(half, which, 2, 3, 3, beside).wait_send()

            @on(parity == 1)
            def _():
                copy(half, which, 2, 1, 1, beside).wait_send()

                @on(lax.rem(which, 2) == 1)
                def _():
                    copy(half, which, 1, 3, 2, ahead).wait_send()
                    copy(half, which, 3, 2, 3, beside).wait_send()


def exchange(record, quality):
    tables = [jnp.asarray(t) for t in half_tables() + (spread_table(), lag_table())]
    anywhere = pl.BlockSpec(memory_space=pl.ANY)
    return pl.pallas_call(
        exchange_kernel,
        out_shape=(
            jax.ShapeDtypeStruct((2, NLAG, CH, CH), F32),
            jax.ShapeDtypeStruct((CH, 2 * FB, 2 * CH), BF),
        ),
        in_specs=[anywhere, pl.BlockSpec(memory_space=pltpu.VMEM)] + [anywhere] * 4,
        out_specs=(anywhere,) * 2,
        scratch_shapes=[
            pltpu.VMEM((CH, LENGTH + HALO), BF),
            pltpu.VMEM((2 * ROWS, HALF), BF),
            pltpu.VMEM((ROWS, 256), BF),
            pltpu.VMEM((CH * 8, 256), BF),
            pltpu.VMEM((NLAG, 2 * FB), BF),
            pltpu.VMEM((GROUPS + 2, 8, CH), F32),
            pltpu.VMEM((GROUPS, 256, CH), BF),
            pltpu.VMEM((GROUPS, 256, CH), BF),
            pltpu.VMEM((3, GROUPS, 256, CH), BF),
            pltpu.VMEM((GROUPS, CH * 8, 256), BF),
            pltpu.VMEM((CH, 2 * FB, 2 * CH), BF),
            pltpu.VMEM((2, CH, 32, 2 * CH), BF),
            pltpu.VMEM((2, 2, NLAG, 8, CH), F32),
            pltpu.SemaphoreType.DMA((4, CHUNKS)),
            pltpu.SemaphoreType.DMA((3, CHUNKS)),
            pltpu.SemaphoreType.DMA((2,)),
            pltpu.SemaphoreType.DMA((2,)),
            pltpu.SemaphoreType.DMA((FRAMES // 2,)),
            pltpu.SemaphoreType.DMA((4,)),
            pltpu.SemaphoreType.DMA((2,)),
        ],
        compiler_params=pltpu.CompilerParams(
            collective_id=0, has_side_effects=True, vmem_limit_bytes=61 * 2**20),
        name="exchange",
    )(record, quality.reshape(1, CH), *tables)


LAST = 16


def last_kernel(lag_ref, near_ref, far_ref, out_ref):
    out_ref[0:2] = near_ref[...]

    @pl.loop(0, LAST // 8)
    def _(step):
        for j in range(8):
            c = step * 8 + j
            result = jnp.dot(lag_ref[...], far_ref[c], preferred_element_type=F32)
            for d in range(2):
                flat = out_ref.at[2 + d].reshape(NLAG * LAST, CH)
                flat[pl.ds(c, NLAG, stride=LAST), :] = result[:, d * CH : (d + 1) * CH]


def last(near, far):
    return pl.pallas_call(
        last_kernel,
        grid=(CH // LAST,),
        out_shape=jax.ShapeDtypeStruct((4, NLAG, CH, CH), F32),
        in_specs=[
            pl.BlockSpec((NLAG, 2 * FB), lambda i: (0, 0)),
            pl.BlockSpec((2, NLAG, LAST, CH), lambda i: (0, 0, i, 0)),
            pl.BlockSpec((LAST, 2 * FB, 2 * CH), lambda i: (i, 0, 0)),
        ],
        out_specs=pl.BlockSpec((4, NLAG, LAST, CH), lambda i: (0, 0, i, 0)),
        compiler_params=pltpu.CompilerParams(vmem_limit_bytes=60 * 2**20),
        name="last",
    )(jnp.asarray(lag_table()), near, far)


def shards(record, quality):
    return last(*exchange(record, quality))[None]


def solution(mesh):
    placed = (P("blk", "pre"), P("blk"))
    return jax.shard_map(
        shards,
        mesh=mesh,
        in_specs=placed,
        out_specs=P("pre", None, None, "blk", None),
        check_vma=False,
    )
```

time: 247 us -> 113 us (0.46)
  waiting for transfers between devices: 138 us -> 0 us
  Pallas kernels: 89.7 us -> 113 us
  local copies, waits for them, and re-layouts: 9.16 us -> 0 us
  starting transfers between devices: 8.27 us -> 0 us
    ppermute x4 -> x0, waiting for transfers between devices: 138 us -> none  [the longest x3 134 us: shards(): lax.ppermute(white, 'blk', [(i, (i + d) % blocks) for i in range(blocks)])]
    pallas_call x2, Pallas kernels: 89.7 us -> 113 us  [the longest x1 95 us: exchange(): pl.pallas_call(exchange_kernel, out_shape=(jax.ShapeDtypeStruct((2, NLAG,...]
    ppermute x4 -> x0, starting transfers between devices: 8.27 us -> none  [the longest x3 6.35 us: shards(): lax.ppermute(white, 'blk', [(i, (i + d) % blocks) for i in range(blocks)])]
    unnamed x16 -> x0, local copies, waits for them, and re-layouts: 8.17 us -> none
  transfers between devices with their start and end apart: 4 -> 0, of which waited for: 4 -> 0; matrix products, arithmetic and copies ran while one was open for 0% -> 0% of each run, Pallas kernels for 0% -> 0%
where the time goes in v3:
time: 113 us
  Pallas kernels  113 us (100%)
    pallas_call x1, Pallas kernels, exchange(): pl.pallas_call(exchange_kernel, out_shape=(jax.ShapeDtypeStruct((2, NLAG,...  95 us
    pallas_call x1, Pallas kernels, last(): pl.pallas_call(last_kernel, grid=(CH // LAST,), out_shape=jax.ShapeDtypeS...  18 us

profile of v3, /device:TPU:16, one launch (start us, length us, event | category | flops | bytes accessed | tf_op | source)
XLA Modules:
  0.0 113.0 jit_solution(16087543315981082725)
XLA Ops:
  0.0 95.0 %exchange.1 = (f32[2,64,128,128]{3,2,1,0:T(8,128)}, bf16[128,256,256]{2,1,0:T(8,128)(2,1)}) custom-call(bf16[128,32768]{1,0:T(8,128)(2,1)} %record_ref.1, s32[1,128]{1,0:T(1,128)} %bitcast.2, bf16[544,1024]{1,0:T(8,128)(2,1)} %constant.8.clone.main_hbm, bf16[272,256]{1,0:T(8,128)(2,1)} %constant.9.clone.tail_hbm, ...), custom_call_target="tpu_custom_call" | custom-call | tf_op jit(solution)/shard_map/exchange/pallas_call | solution.py:404
  95.0 18.0 %last.1 = f32[4,64,128,128]{3,2,1,0:T(8,128)} custom-call(bf16[64,256]{1,0:T(8,128)(2,1)} %constant.11.clone.lag_hbm.lag_ref, f32[2,64,128,128]{3,2,1,0:T(8,128)} %get-tuple-element.7.near_ref, bf16[128,256,256]{2,1,0:T(8,128)(2,1)} %get-tuple-element.8.far_ref), custom_call_target="tpu_custom_call" | custom-call | tf_op jit(solution)/shard_map/last/pallas_call | solution.py:457

commit v4 on v3

--- a/solution.py
+++ b/solution.py
@@ -77,11 +77,20 @@
 CHUNKS = 16
 PART = 32
 LENGTH = FRAMES * HALF
+LAST = 16
+
+
+def lags(lag, cross, which, target):
+    for j in range(LAST):
+        result = jnp.dot(lag[...], cross[which * LAST + j], preferred_element_type=F32)
+        for d in range(2):
+            flat = target.at[d].reshape(NLAG * LAST, CH)
+            flat[pl.ds(j, NLAG, stride=LAST), :] = result[:, d * CH : (d + 1) * CH]
 
 
 def exchange_kernel(record_ref, quality_ref, main_hbm, tail_hbm, spread_hbm, lag_hbm, near_ref, far_ref,
-                    rec, main, tail, spread, lag, held, white, turned, got, left, cross, fars, nears,
-                    send_sem, recv_sem, far_sem, near_sem, rec_sem, table_sem, halo_sem):
+                    rec, main, tail, spread, lag, held, white, turned, got, left,
+                    send_sem, recv_sem, rec_sem, table_sem, halo_sem):
     tables = [
         pltpu.make_async_copy(source, target, table_sem.at[i])
         for i, (source, target) in enumerate(
@@ -307,68 +316,30 @@
                     jnp.dot(left[group, lines, :], right, preferred_element_type=F32).reshape(PART, 8, 2 * CH))
             store(part, jnp.concatenate(pieces, 1).astype(BF))
 
-    @pl.loop(0, 8)
-    def _(which):
-        relay(1, which)
-
+    def fill(which, one, two):
         @pl.loop(0, 2)
         def _(j):
             pair = which * 2 + j
 
             def store(part, value):
-                cross[pl.ds(part * PART, PART), pl.ds(pl.multiple_of(pair * 16, 16), 16), :] = value
-
-            products(pair, white, got.at[0], store)
-
-    def store_far(which):
-        at = pl.ds(pl.multiple_of(which * 32, 32), 32)
-        buffer = lax.rem(which, 2)
-        return pltpu.make_async_copy(fars.at[buffer], far_ref.at[:, at, :], far_sem.at[buffer])
-
-    def store_near(which):
-        at = pl.ds(pl.multiple_of(which * 8, 8), 8)
-        buffer = lax.rem(which, 2)
-        return pltpu.make_async_copy(nears.at[buffer], near_ref.at[:, :, at, :], near_sem.at[buffer])
+                far_ref[pl.ds(part * PART, PART), pl.ds(pl.multiple_of(pair * 16, 16), 16), :] = value
+
+            products(pair, one, two, store)
 
     @pl.loop(0, 8)
     def _(which):
+        relay(1, which)
+        fill(which, white, got.at[0])
+
+    @pl.loop(0, 8)
+    def _(which):
         finish(0, which)
-        for buffer in range(2):
-            step = which * 2 + buffer
-
-            @on(which > 0)
-            def _():
-                store_near(step - 2).wait()
-
-            for j in range(8):
-                result = jnp.dot(lag[...], cross[step * 8 + j], preferred_element_type=F32)
-                for d in range(2):
-                    flat = nears.at[buffer, d].reshape(NLAG * 8, CH)
-                    flat[pl.ds(j, NLAG, stride=8), :] = result[:, d * CH : (d + 1) * CH]
-            store_near(step).start()
+        lags(lag, far_ref, which, near_ref.at[which])
 
     @pl.loop(0, 8)
     def _(which):
         finish(1, which)
-
-        @on(which > 1)
-        def _():
-            store_far(which - 2).wait()
-
-        @pl.loop(0, 2)
-        def _(j):
-            def store(part, value):
-                fars[lax.rem(which, 2), pl.ds(part * PART, PART),
-                     pl.ds(pl.multiple_of(j * 16, 16), 16), :] = value
-
-            products(which * 2 + j, got.at[1], got.at[2], store)
-
-        store_far(which).start()
-
-    for step in (CHUNKS - 2, CHUNKS - 1):
-        store_near(step).wait()
-    for which in (6, 7):
-        store_far(which).wait()
+        fill(which, got.at[1], got.at[2])
 
     @on(segment > 0)
     def _():
@@ -404,11 +375,11 @@
     return pl.pallas_call(
         exchange_kernel,
         out_shape=(
-            jax.ShapeDtypeStruct((2, NLAG, CH, CH), F32),
-            jax.ShapeDtypeStruct((CH, 2 * FB, 2 * CH), BF),
+            pltpu.VMEM((CH // LAST, 2, NLAG, LAST, CH), F32),
+            pltpu.VMEM((CH, 2 * FB, 2 * CH), BF),
         ),
         in_specs=[anywhere, pl.BlockSpec(memory_space=pltpu.VMEM)] + [anywhere] * 4,
-        out_specs=(anywhere,) * 2,
+        out_specs=(pl.BlockSpec(memory_space=pltpu.VMEM),) * 2,
         scratch_shapes=[
             pltpu.VMEM((CH, LENGTH + HALO), BF),
             pltpu.VMEM((2 * ROWS, HALF), BF),
@@ -420,51 +391,62 @@
             pltpu.VMEM((GROUPS, 256, CH), BF),
             pltpu.VMEM((3, GROUPS, 256, CH), BF),
             pltpu.VMEM((GROUPS, CH * 8, 256), BF),
-            pltpu.VMEM((CH, 2 * FB, 2 * CH), BF),
-            pltpu.VMEM((2, CH, 32, 2 * CH), BF),
-            pltpu.VMEM((2, 2, NLAG, 8, CH), F32),
             pltpu.SemaphoreType.DMA((4, CHUNKS)),
             pltpu.SemaphoreType.DMA((3, CHUNKS)),
-            pltpu.SemaphoreType.DMA((2,)),
-            pltpu.SemaphoreType.DMA((2,)),
             pltpu.SemaphoreType.DMA((FRAMES // 2,)),
             pltpu.SemaphoreType.DMA((4,)),
             pltpu.SemaphoreType.DMA((2,)),
         ],
         compiler_params=pltpu.CompilerParams(
-            collective_id=0, has_side_effects=True, vmem_limit_bytes=61 * 2**20),
+            collective_id=0, has_side_effects=True, vmem_limit_bytes=38 * 2**20),
         name="exchange",
     )(record, quality.reshape(1, CH), *tables)
 
 
-LAST = 16
-
-
-def last_kernel(lag_ref, near_ref, far_ref, out_ref):
-    out_ref[0:2] = near_ref[...]
-
-    @pl.loop(0, LAST // 8)
-    def _(step):
-        for j in range(8):
-            c = step * 8 + j
-            result = jnp.dot(lag_ref[...], far_ref[c], preferred_element_type=F32)
-            for d in range(2):
-                flat = out_ref.at[2 + d].reshape(NLAG * LAST, CH)
-                flat[pl.ds(c, NLAG, stride=LAST), :] = result[:, d * CH : (d + 1) * CH]
+def last_kernel(lag, near, far, out_ref, staged, near_sem, far_sem):
+    def store_near(which):
+        at = pl.ds(pl.multiple_of(which * LAST, LAST), LAST)
+        return pltpu.make_async_copy(near.at[which], out_ref.at[pl.ds(0, 2), :, at, :], near_sem.at[which])
+
+    def store_far(which):
+        at = pl.ds(pl.multiple_of(which * LAST, LAST), LAST)
+        buffer = lax.rem(which, 2)
+        return pltpu.make_async_copy(staged.at[buffer], out_ref.at[pl.ds(2, 2), :, at, :], far_sem.at[buffer])
+
+    steps = CH // LAST
+
+    @pl.loop(0, steps)
+    def _(which):
+        store_near(which).start()
+
+        @pl.when(which > 1)
+        def _():
+            store_far(which - 2).wait()
+
+        lags(lag, far, which, staged.at[lax.rem(which, 2)])
+        store_far(which).start()
+
+    for which in (steps - 2, steps - 1):
+        store_far(which).wait()
+
+    @pl.loop(0, steps)
+    def _(which):
+        store_near(which).wait()
 
 
 def last(near, far):
+    inside = pl.BlockSpec(memory_space=pltpu.VMEM)
     return pl.pallas_call(
         last_kernel,
-        grid=(CH // LAST,),
         out_shape=jax.ShapeDtypeStruct((4, NLAG, CH, CH), F32),
-        in_specs=[
-            pl.BlockSpec((NLAG, 2 * FB), lambda i: (0, 0)),
-            pl.BlockSpec((2, NLAG, LAST, CH), lambda i: (0, 0, i, 0)),
-            pl.BlockSpec((LAST, 2 * FB, 2 * CH), lambda i: (i, 0, 0)),
+        in_specs=[inside] * 3,
+        out_specs=pl.BlockSpec(memory_space=pl.ANY),
+        scratch_shapes=[
+            pltpu.VMEM((2, 2, NLAG, LAST, CH), F32),
+            pltpu.SemaphoreType.DMA((CH // LAST,)),
+            pltpu.SemaphoreType.DMA((2,)),
         ],
-        out_specs=pl.BlockSpec((4, NLAG, LAST, CH), lambda i: (0, 0, i, 0)),
-        compiler_params=pltpu.CompilerParams(vmem_limit_bytes=60 * 2**20),
+        compiler_params=pltpu.CompilerParams(vmem_limit_bytes=8 * 2**20),
         name="last",
     )(jnp.asarray(lag_table()), near, far)
 

time: 113 us -> 99.8 us (0.88)
  Pallas kernels: 113 us -> 99.6 us
    pallas_call x2, Pallas kernels: 113 us -> 99.6 us  [the longest x1 92.5 us: exchange(): pl.pallas_call(exchange_kernel, out_shape=(pltpu.VMEM((CH // LAST, 2, NLA...]
where the time goes in v4:
time: 99.8 us; the launch traced here: 99.6 us
  Pallas kernels  99.6 us (100%)
    pallas_call x1, Pallas kernels, exchange(): pl.pallas_call(exchange_kernel, out_shape=(pltpu.VMEM((CH // LAST, 2, NLA...  92.5 us
    pallas_call x1, Pallas kernels, last(): pl.pallas_call(last_kernel, out_shape=jax.ShapeDtypeStruct((4, NLAG, CH,...  7.1 us

profile of v4, /device:TPU:16, one launch (start us, length us, event | category | flops | bytes accessed | tf_op | source)
XLA Modules:
  0.0 99.6 jit_solution(17328534983803721312)
XLA Ops:
  0.0 0.0 copy-start
  0.0 92.5 %exchange.1 = (f32[8,2,64,16,128]{4,3,2,1,0:T(8,128)S(1)}, bf16[128,256,256]{2,1,0:T(8,128)(2,1)S(1)}) custom-call(bf16[128,32768]{1,0:T(8,128)(2,1)} %record_ref.1, s32[1,128]{1,0:T(1,128)} %bitcast.2, bf16[544,1024]{1,0:T(8,128)(2,1)} %constant.8.clone.main_hbm, bf16[272,256]{1,0:T(8,128)(2,1)} %constant.9.clone.tail_hbm, ...), custom_call_target="tpu_custom_call" | custom-call | tf_op jit(solution)/shard_map/exchange/pallas_call | solution.py:375
  92.5 0.0 copy-done
  92.5 7.1 %last.1 = f32[4,64,128,128]{3,2,1,0:T(8,128)} custom-call(bf16[64,256]{1,0:T(8,128)(2,1)S(1)} %copy-done, f32[8,2,64,16,128]{4,3,2,1,0:T(8,128)S(1)} %get-tuple-element.7.near, bf16[128,256,256]{2,1,0:T(8,128)(2,1)S(1)} %get-tuple-element.8.far), custom_call_target="tpu_custom_call" | custom-call | tf_op jit(solution)/shard_map/last/pallas_call | solution.py:439
Async XLA Ops:
  0.0 92.5 %copy-start = (bf16[64,256]{1,0:T(8,128)(2,1)S(1)}, bf16[64,256]{1,0:T(8,128)(2,1)}, u32[]{:S(2)}) copy-start(bf16[64,256]{1,0:T(8,128)(2,1)} %constant.11.clone.lag_hbm.lag) | copy-start | bytes 98308

commit v5 on v4

--- a/solution.py
+++ b/solution.py
@@ -80,6 +80,164 @@
 LAST = 16
 
 
+KINDS = [5, 6, 3, 5, 6, 2, 2, 2, 7, 3, 4, 2, 3, 3, 7, 4]
+OWN = {
+    0: {2: [("y", 1), ("z", 2)], 3: [("y", 1)], 4: [("y", 1)], 5: [("d", 4), ("y", 1)],
+        6: [("y", 1), ("z", 2)], 7: [("d", 4), ("y", 1)]},
+    1: {kind: [("z", 2)] for kind in range(2, 8)},
+}
+ONWARD = {
+    0: {
+        2: {1: ("z", 3), 2: ("y", 3)},
+        3: {1: ("z", 3)},
+        4: {1: ("z", 3)},
+        5: {1: ("z", 3), 2: ("y", 3), 4: ("d", 5), 5: ("e", 2)},
+        6: {1: ("z", 3)},
+        7: {1: ("z", 3), 4: ("d", 5), 5: ("e", 2)},
+    },
+    1: {
+        2: {2: ("y", 1)},
+        3: {2: ("y", 1), 1: ("z", 3), 3: ("y", 2)},
+        4: {2: ("y", 1), 1: ("d", 4), 4: ("d", 5), 5: ("e", 3), 3: ("y", 2)},
+        5: {2: ("y", 1)},
+        6: {2: ("y", 1), 1: ("d", 4), 4: ("d", 5), 5: ("e", 3)},
+        7: {2: ("y", 1), 1: ("z", 3)},
+    },
+}
+ARRIVALS = (
+    [
+        [],
+        [],
+        [],
+        [],
+        [],
+        [],
+        [(4, 0)],
+        [(2, 1)],
+        [],
+        [(4, 3)],
+        [(2, 4)],
+        [(1, 0)],
+        [(5, 0)],
+        [(2, 5)],
+        [],
+        [(1, 1), (5, 3)],
+        [(2, 6), (1, 2)],
+        [(2, 0)],
+        [],
+        [(2, 7)],
+        [],
+        [(1, 3)],
+        [(2, 3)],
+        [],
+        [(3, 0)],
+        [],
+        [(1, 4)],
+        [(4, 8)],
+        [],
+        [(3, 1)],
+        [],
+        [(1, 5)],
+        [(4, 14), (2, 11), (1, 6), (5, 8), (3, 2), (1, 7), (5, 14), (3, 3), (2, 2), (2, 8), (3, 4), (1, 8)],
+        [(2, 14), (3, 5), (1, 9)],
+        [(3, 6), (1, 10)],
+        [(3, 7), (1, 11)],
+        [(3, 8), (1, 12)],
+        [(3, 9), (1, 13)],
+        [(3, 10), (1, 14)],
+        [(3, 11), (1, 15)],
+        [],
+        [(3, 12)],
+        [],
+        [(2, 10)],
+        [(3, 13)],
+        [],
+        [(2, 9)],
+        [],
+        [(3, 14)],
+        [(2, 12)],
+        [(3, 15)],
+        [],
+        [(2, 13)],
+        [],
+        [(2, 15)],
+        [],
+        [],
+    ],
+    [
+        [],
+        [],
+        [],
+        [],
+        [],
+        [],
+        [(1, 0), (2, 0)],
+        [],
+        [],
+        [(1, 1), (2, 1)],
+        [],
+        [],
+        [(1, 2), (2, 2)],
+        [],
+        [],
+        [(4, 1), (1, 3), (2, 3)],
+        [],
+        [(1, 4), (2, 4)],
+        [],
+        [],
+        [],
+        [(5, 1)],
+        [(1, 5), (2, 5)],
+        [],
+        [],
+        [],
+        [(4, 4)],
+        [(1, 6), (2, 6)],
+        [],
+        [],
+        [],
+        [(3, 1)],
+        [(1, 7), (2, 7), (5, 4), (3, 2), (3, 5), (1, 8), (2, 8)],
+        [(3, 4), (1, 9), (2, 9)],
+        [(1, 10), (2, 10)],
+        [(1, 11), (2, 11)],
+        [(4, 10), (1, 12), (2, 12)],
+        [(1, 13), (2, 13)],
+        [(5, 10), (1, 14), (2, 14)],
+        [(1, 15), (2, 15)],
+        [(3, 10)],
+        [],
+        [(3, 6), (3, 8)],
+        [],
+        [],
+        [(4, 15)],
+        [(3, 0), (3, 9)],
+        [],
+        [(3, 7), (3, 12), (5, 15), (3, 3), (3, 13)],
+        [],
+        [],
+        [(3, 11), (3, 14), (3, 15)],
+        [],
+        [],
+        [],
+        [],
+        [],
+    ],
+)
+PASSING = {0: (5, 7), 1: (4, 6)}
+
+
+def sends_of(parity, chunk):
+    kind = KINDS[chunk]
+    return [(0,) + way for way in OWN[parity][kind]] + [
+        (buffer,) + way for buffer, way in sorted(ONWARD[parity][kind].items())]
+
+
+def passing_place(parity, chunk):
+    first = chunk - chunk % 8
+    return sum(KINDS[c] in PASSING[parity] for c in range(first, chunk))
+
+
 def lags(lag, cross, which, target):
     for j in range(LAST):
         result = jnp.dot(lag[...], cross[which * LAST + j], preferred_element_type=F32)
@@ -89,7 +247,7 @@
 
 
 def exchange_kernel(record_ref, quality_ref, main_hbm, tail_hbm, spread_hbm, lag_hbm, near_ref, far_ref,
-                    rec, main, tail, spread, lag, held, white, turned, got, left,
+                    rec, main, tail, spread, lag, held, white, turned, got, early, late, left,
                     send_sem, recv_sem, rec_sem, table_sem, halo_sem):
     tables = [
         pltpu.make_async_copy(source, target, table_sem.at[i])
@@ -115,16 +273,24 @@
     behind = lax.rem(me + count - 2, count)
     parity = lax.rem(me, 2)
     beside = me + 1 - 2 * parity
+    column = lax.div(me, 2)
+    x, z = lax.div(column, 4), lax.rem(column, 4)
+    columns = lax.div(count, 2)
+    below = 2 * (x * 4 + lax.rem(z + 3, 4)) + parity
+    above = 2 * (x * 4 + lax.rem(z + 1, 4)) + parity
+    target = 2 * lax.rem(x * 4 + lax.rem(z + 2, 4) + 1, columns) + parity
+    origin = lax.rem(column + columns - 1, columns)
+    source_of_me = 2 * (lax.div(origin, 4) * 4 + lax.rem(lax.rem(origin, 4) + 2, 4)) + parity
     segment = lax.axis_index("pre")
     segments = lax.axis_size("pre")
     sooner = lax.rem(segment + segments - 1, segments)
     later = lax.rem(segment + 1, segments)
     barrier = pltpu.get_barrier_semaphore()
-    for other in (ahead, behind, beside):
+    for other in (ahead, behind, beside, below, above, target, source_of_me):
         pl.semaphore_signal(barrier, inc=1, device_id={"blk": other}, device_id_type=pl.DeviceIdType.MESH)
     for other in (sooner, later):
         pl.semaphore_signal(barrier, inc=1, device_id={"pre": other}, device_id_type=pl.DeviceIdType.MESH)
-    pl.semaphore_wait(barrier, 5)
+    pl.semaphore_wait(barrier, 9)
 
     halo = pltpu.make_async_remote_copy(
         src_ref=record_ref.at[:, pl.ds(0, HALO)],
@@ -143,73 +309,64 @@
     def _():
         rec[:, LENGTH:] = jnp.zeros((CH, HALO), BF)
 
-    def view(ref, half, which):
+    devices = {"y": beside, "z": ahead, "d": below, "e": target}
+
+    def view(buffer, side, chunk):
+        half, which = divmod(chunk, 8)
+        if buffer > 3:
+            return (early, late)[half].at[buffer - 4, passing_place(side, chunk)]
+        ref = white if buffer == 0 else got.at[buffer - 1]
         if half == 0:
-            return ref.at[:, pl.ds(pl.multiple_of(which * 16, 16), 16), :]
+            return ref.at[:, pl.ds(which * 16, 16), :]
         return ref.at[pl.ds(which * 4, 4), pl.ds(128, 128), :]
 
-    def copy(half, which, source, target, slot, device):
+    def copy(side, chunk, buffer, way, there):
+        slot = sends_of(side, chunk).index((buffer, way, there))
         return pltpu.make_async_remote_copy(
-            src_ref=view(white if source == 0 else got.at[source - 1], half, which),
-            dst_ref=view(got.at[target - 1], half, which),
-            send_sem=send_sem.at[slot, half * 8 + which],
-            recv_sem=recv_sem.at[target - 1, half * 8 + which],
-            device_id={"blk": device},
+            src_ref=view(buffer, side, chunk),
+            dst_ref=view(there, side, chunk),
+            send_sem=send_sem.at[slot, chunk],
+            recv_sem=recv_sem.at[there - 1, chunk],
+            device_id={"blk": devices[way]},
             device_id_type=pl.DeviceIdType.MESH,
         )
 
-    def arrived(half, which, source):
-        copy(half, which, 0, source, 0, beside).wait_recv()
+    def landed(side, chunk, buffer):
+        return pltpu.make_async_remote_copy(
+            src_ref=view(buffer, side, chunk),
+            dst_ref=view(buffer, side, chunk),
+            send_sem=send_sem.at[0, chunk],
+            recv_sem=recv_sem.at[buffer - 1, chunk],
+            device_id={"blk": beside},
+            device_id_type=pl.DeviceIdType.MESH,
+        )
 
     def on(condition):
         return lambda body: pl.when(condition)(body)
 
-    def offer(half, which):
-        @on(parity == 0)
-        def _():
-            copy(half, which, 0, 1, 0, beside).start()
-
-            @on(lax.rem(which, 2) == 0)
+    def offer(side, chunk):
+        for way, there in OWN[side][KINDS[chunk]]:
+            copy(side, chunk, 0, way, there).start()
+
+    def each_side(body):
+        for side in range(2):
+            @on(parity == side)
             def _():
-                copy(half, which, 0, 2, 1, ahead).start()
-
-        @on(parity == 1)
-        def _():
-            copy(half, which, 0, 2, 0, ahead).start()
-
-    def relay(half, which):
-        @on(parity == 0)
-        def _():
-            arrived(half, which, 1)
-            copy(half, which, 1, 3, 2, ahead).start()
-
-            @on(lax.rem(which, 2) == 0)
-            def _():
-                arrived(half, which, 2)
-                copy(half, which, 2, 3, 3, beside).start()
-
-        @on(parity == 1)
-        def _():
-            arrived(half, which, 2)
-            copy(half, which, 2, 1, 1, beside).start()
-            arrived(half, which, 1)
-
-            @on(lax.rem(which, 2) == 1)
-            def _():
-                copy(half, which, 1, 3, 2, ahead).start()
-
-    def finish(half, which):
-        arrived(half, which, 3)
-
-        @on(lax.rem(which, 2) == 1)
-        def _():
-            @on(parity == 0)
-            def _():
-                arrived(half, which, 2)
-
-            @on(parity == 1)
-            def _():
-                copy(half, which, 3, 2, 3, beside).start()
+                body(side)
+
+    def visit(piece_at, step, steps):
+        def body(side):
+            for i in range(steps):
+                if ARRIVALS[side][piece_at + i]:
+                    @on(step == i)
+                    def _():
+                        for buffer, chunk in ARRIVALS[side][piece_at + i]:
+                            landed(side, chunk, buffer).wait_recv()
+                            onward = ONWARD[side][KINDS[chunk]].get(buffer)
+                            if onward:
+                                copy(side, chunk, buffer, *onward).start()
+
+        each_side(body)
 
     def transform(raw, after):
         both = lax.dot_general(main[...], raw, NT, preferred_element_type=F32)
@@ -258,14 +415,10 @@
         white[:, at, :] = jnp.concatenate([w0, w1], 1).astype(BF)
         turned[:, at, :] = jnp.concatenate([t0, t1], 1).astype(BF)
 
-    @pl.loop(0, 8)
+    @pl.loop(0, FRAMES // 2)
     def _(step):
-        piece(step + 1).wait()
-        frames(step)
-        offer(0, step)
-
-    @pl.loop(8, FRAMES // 2)
-    def _(step):
+        visit(0, step, 16)
+
         @on(step < FRAMES // 2 - 1)
         def _():
             piece(step + 1).wait()
@@ -276,13 +429,19 @@
 
         frames(step)
 
-        @on(lax.rem(step, 3) == 0)
-        def _():
-            relay(0, lax.div(step, 3) - 3)
-
-    @pl.loop(0, 8)
-    def _(which):
-        offer(1, which)
+        def body(side):
+            for i in range(8):
+                @on(step == i)
+                def _():
+                    offer(side, i)
+
+        each_side(body)
+
+    def rest(side):
+        for chunk in range(8, CHUNKS):
+            offer(side, chunk)
+
+    each_side(rest)
 
     tables[2].wait()
     tables[3].wait()
@@ -290,20 +449,16 @@
     cols = lax.broadcasted_iota(jnp.int32, (PART * 8, 256), 1)
     diagonal = (rows % 4) == (cols % 4)
 
-    @pl.loop(3, 8)
-    def _(which):
-        relay(0, which)
-
-        @on(which < 7)
-        def _():
-            @pl.loop(0, 8)
-            def _(j):
-                group = (which - 3) * 8 + j
-                own = jnp.concatenate([white[group], turned[group]], 1)
-                for part in range(CH // PART):
-                    lines = pl.ds(part * PART * 8, PART * 8)
-                    table = lax.dot_general(spread[lines, :], own, NT, preferred_element_type=F32)
-                    left[group, lines, :] = jnp.where(diagonal, table, 0.0).astype(BF)
+    @pl.loop(0, GROUPS // 2)
+    def _(step):
+        visit(16, step, 16)
+        for j in range(2):
+            group = step * 2 + j
+            own = jnp.concatenate([white[group], turned[group]], 1)
+            for part in range(CH // PART):
+                lines = pl.ds(part * PART * 8, PART * 8)
+                table = lax.dot_general(spread[lines, :], own, NT, preferred_element_type=F32)
+                left[group, lines, :] = jnp.where(diagonal, table, 0.0).astype(BF)
 
     def products(pair, one, two, store):
         for part in range(CH // PART):
@@ -328,45 +483,31 @@
 
     @pl.loop(0, 8)
     def _(which):
-        relay(1, which)
+        visit(32, which, 8)
         fill(which, white, got.at[0])
 
     @pl.loop(0, 8)
     def _(which):
-        finish(0, which)
+        visit(40, which, 8)
         lags(lag, far_ref, which, near_ref.at[which])
 
     @pl.loop(0, 8)
     def _(which):
-        finish(1, which)
+        visit(48, which, 8)
         fill(which, got.at[1], got.at[2])
+
+    visit(56, 0, 1)
 
     @on(segment > 0)
     def _():
         halo.wait_send()
 
-    for half in range(2):
-        @pl.loop(0, 8)
-        def _(which):
-            copy(half, which, 0, 1, 0, beside).wait_send()
-
-            @on(parity == 0)
-            def _():
-                copy(half, which, 1, 3, 2, ahead).wait_send()
-
-                @on(lax.rem(which, 2) == 0)
-                def _():
-                    copy(half, which, 0, 2, 1, ahead).wait_send()
-                    copy(half, which, 2, 3, 3, beside).wait_send()
-
-            @on(parity == 1)
-            def _():
-                copy(half, which, 2, 1, 1, beside).wait_send()
-
-                @on(lax.rem(which, 2) == 1)
-                def _():
-                    copy(half, which, 1, 3, 2, ahead).wait_send()
-                    copy(half, which, 3, 2, 3, beside).wait_send()
+    def sent(side):
+        for chunk in range(CHUNKS):
+            for buffer, way, there in sends_of(side, chunk):
+                copy(side, chunk, buffer, way, there).wait_send()
+
+    each_side(sent)
 
 
 def exchange(record, quality):
@@ -390,15 +531,17 @@
             pltpu.VMEM((GROUPS, 256, CH), BF),
             pltpu.VMEM((GROUPS, 256, CH), BF),
             pltpu.VMEM((3, GROUPS, 256, CH), BF),
+            pltpu.VMEM((2, 2, GROUPS, 16, CH), BF),
+            pltpu.VMEM((2, 2, 4, 128, CH), BF),
             pltpu.VMEM((GROUPS, CH * 8, 256), BF),
-            pltpu.SemaphoreType.DMA((4, CHUNKS)),
-            pltpu.SemaphoreType.DMA((3, CHUNKS)),
+            pltpu.SemaphoreType.DMA((6, CHUNKS)),
+            pltpu.SemaphoreType.DMA((5, CHUNKS)),
             pltpu.SemaphoreType.DMA((FRAMES // 2,)),
             pltpu.SemaphoreType.DMA((4,)),
             pltpu.SemaphoreType.DMA((2,)),
         ],
         compiler_params=pltpu.CompilerParams(
-            collective_id=0, has_side_effects=True, vmem_limit_bytes=38 * 2**20),
+            collective_id=0, has_side_effects=True, vmem_limit_bytes=39 * 2**20),
         name="exchange",
     )(record, quality.reshape(1, CH), *tables)
 

time: 99.8 us -> 92.4 us (0.926)
  Pallas kernels: 99.6 us -> 92.2 us
    pallas_call x1, Pallas kernels: 92.5 us -> 85.1 us  [exchange(): pl.pallas_call(exchange_kernel, out_shape=(pltpu.VMEM((CH // LAST, 2, NLA...]
where the time goes in v5:
time: 92.4 us; the launch traced here: 92.2 us
  Pallas kernels  92.2 us (100%)
    pallas_call x1, Pallas kernels, exchange(): pl.pallas_call(exchange_kernel, out_shape=(pltpu.VMEM((CH // LAST, 2, NLA...  85.1 us
    pallas_call x1, Pallas kernels, last(): pl.pallas_call(last_kernel, out_shape=jax.ShapeDtypeStruct((4, NLAG, CH,...  7.1 us

profile of v5, /device:TPU:16, one launch (start us, length us, event | category | flops | bytes accessed | tf_op | source)
XLA Modules:
  0.0 92.2 jit_solution(12114653418535562388)
XLA Ops:
  0.0 0.0 copy-start
  0.0 85.1 %exchange.1 = (f32[8,2,64,16,128]{4,3,2,1,0:T(8,128)S(1)}, bf16[128,256,256]{2,1,0:T(8,128)(2,1)S(1)}) custom-call(bf16[128,32768]{1,0:T(8,128)(2,1)} %record_ref.1, s32[1,128]{1,0:T(1,128)} %bitcast.2, bf16[544,1024]{1,0:T(8,128)(2,1)} %constant.8.clone.main_hbm, bf16[272,256]{1,0:T(8,128)(2,1)} %constant.9.clone.tail_hbm, ...), custom_call_target="tpu_custom_call" | custom-call | tf_op jit(solution)/shard_map/exchange/pallas_call | solution.py:516
  85.1 0.0 copy-done
  85.1 7.1 %last.1 = f32[4,64,128,128]{3,2,1,0:T(8,128)} custom-call(bf16[64,256]{1,0:T(8,128)(2,1)S(1)} %copy-done, f32[8,2,64,16,128]{4,3,2,1,0:T(8,128)S(1)} %get-tuple-element.7.near, bf16[128,256,256]{2,1,0:T(8,128)(2,1)S(1)} %get-tuple-element.8.far), custom_call_target="tpu_custom_call" | custom-call | tf_op jit(solution)/shard_map/last/pallas_call | solution.py:582
Async XLA Ops:
  0.0 85.1 %copy-start = (bf16[64,256]{1,0:T(8,128)(2,1)S(1)}, bf16[64,256]{1,0:T(8,128)(2,1)}, u32[]{:S(2)}) copy-start(bf16[64,256]{1,0:T(8,128)(2,1)} %constant.11.clone.lag_hbm.lag) | copy-start | bytes 98308

commit v6 on v5

--- a/solution.py
+++ b/solution.py
@@ -80,7 +80,7 @@
 LAST = 16
 
 
-KINDS = [5, 6, 3, 5, 6, 2, 2, 2, 7, 3, 4, 2, 3, 3, 7, 4]
+KINDS = [2, 5, 6, 6, 3, 7, 6, 7, 4, 4, 2, 2, 5, 3, 3, 7]
 OWN = {
     0: {2: [("y", 1), ("z", 2)], 3: [("y", 1)], 4: [("y", 1)], 5: [("d", 4), ("y", 1)],
         6: [("y", 1), ("z", 2)], 7: [("d", 4), ("y", 1)]},
@@ -112,55 +112,55 @@
         [],
         [],
         [],
-        [(4, 0)],
-        [(2, 1)],
-        [],
-        [(4, 3)],
-        [(2, 4)],
-        [(1, 0)],
-        [(5, 0)],
-        [(2, 5)],
-        [],
-        [(1, 1), (5, 3)],
-        [(2, 6), (1, 2)],
         [(2, 0)],
-        [],
-        [(2, 7)],
-        [],
-        [(1, 3)],
+        [(4, 1)],
+        [],
+        [(2, 2)],
+        [],
+        [(4, 5), (1, 0)],
         [(2, 3)],
         [],
+        [(5, 1)],
+        [(1, 1), (2, 6)],
+        [(4, 7), (1, 2)],
         [(3, 0)],
         [],
-        [(1, 4)],
-        [(4, 8)],
-        [],
+        [],
+        [],
+        [(5, 5), (1, 3)],
         [(3, 1)],
         [],
-        [(1, 5)],
-        [(4, 14), (2, 11), (1, 6), (5, 8), (3, 2), (1, 7), (5, 14), (3, 3), (2, 2), (2, 8), (3, 4), (1, 8)],
-        [(2, 14), (3, 5), (1, 9)],
-        [(3, 6), (1, 10)],
-        [(3, 7), (1, 11)],
-        [(3, 8), (1, 12)],
-        [(3, 9), (1, 13)],
-        [(3, 10), (1, 14)],
-        [(3, 11), (1, 15)],
-        [],
-        [(3, 12)],
-        [],
+        [],
+        [],
+        [(2, 1), (1, 4)],
         [(2, 10)],
-        [(3, 13)],
-        [],
-        [(2, 9)],
-        [],
-        [(3, 14)],
-        [(2, 12)],
-        [(3, 15)],
-        [],
-        [(2, 13)],
-        [],
-        [(2, 15)],
+        [],
+        [],
+        [],
+        [(4, 12), (1, 5)],
+        [(2, 11), (4, 15), (1, 6), (3, 2), (5, 7), (1, 7), (3, 3), (2, 5), (1, 8)],
+        [(3, 4), (5, 12), (1, 9)],
+        [(3, 5), (5, 15), (1, 10)],
+        [(3, 6), (2, 7), (1, 11)],
+        [(3, 7), (2, 12), (1, 12)],
+        [(3, 8), (2, 15), (1, 13)],
+        [(3, 9), (1, 14)],
+        [(3, 10), (1, 15)],
+        [(3, 11)],
+        [],
+        [],
+        [(2, 4), (3, 12)],
+        [],
+        [],
+        [(2, 8), (3, 13)],
+        [],
+        [],
+        [(2, 9), (3, 14)],
+        [],
+        [],
+        [(2, 13), (3, 15)],
+        [],
+        [(2, 14)],
         [],
         [],
     ],
@@ -180,46 +180,46 @@
         [(1, 2), (2, 2)],
         [],
         [],
-        [(4, 1), (1, 3), (2, 3)],
-        [],
+        [(1, 3), (2, 3)],
+        [(4, 2)],
         [(1, 4), (2, 4)],
         [],
         [],
         [],
-        [(5, 1)],
+        [(4, 3)],
         [(1, 5), (2, 5)],
         [],
         [],
         [],
-        [(4, 4)],
-        [(1, 6), (2, 6)],
-        [],
-        [],
-        [],
-        [(3, 1)],
-        [(1, 7), (2, 7), (5, 4), (3, 2), (3, 5), (1, 8), (2, 8)],
-        [(3, 4), (1, 9), (2, 9)],
-        [(1, 10), (2, 10)],
-        [(1, 11), (2, 11)],
-        [(4, 10), (1, 12), (2, 12)],
-        [(1, 13), (2, 13)],
-        [(5, 10), (1, 14), (2, 14)],
-        [(1, 15), (2, 15)],
-        [(3, 10)],
-        [],
-        [(3, 6), (3, 8)],
-        [],
-        [],
-        [(4, 15)],
-        [(3, 0), (3, 9)],
-        [],
-        [(3, 7), (3, 12), (5, 15), (3, 3), (3, 13)],
-        [],
-        [],
-        [(3, 11), (3, 14), (3, 15)],
-        [],
-        [],
-        [],
+        [(5, 2)],
+        [(2, 6), (3, 0)],
+        [],
+        [],
+        [],
+        [(5, 3)],
+        [(1, 6), (2, 7), (3, 2), (1, 7), (2, 8), (3, 3), (1, 8), (2, 9)],
+        [(4, 6), (1, 9), (2, 10)],
+        [(4, 8), (1, 10), (2, 11)],
+        [(5, 6), (1, 11), (2, 12)],
+        [(4, 9), (1, 12), (2, 13)],
+        [(5, 8), (1, 13), (2, 14)],
+        [(3, 6), (1, 14), (2, 15)],
+        [(5, 9), (1, 15), (3, 4)],
+        [],
+        [],
+        [(3, 8), (3, 1), (3, 5)],
+        [],
+        [],
+        [(3, 9)],
+        [(3, 7), (3, 10)],
+        [],
+        [],
+        [(3, 11), (3, 13)],
+        [],
+        [(3, 12), (3, 14)],
+        [],
+        [],
+        [(3, 15)],
         [],
         [],
     ],
@@ -531,8 +531,8 @@
             pltpu.VMEM((GROUPS, 256, CH), BF),
             pltpu.VMEM((GROUPS, 256, CH), BF),
             pltpu.VMEM((3, GROUPS, 256, CH), BF),
-            pltpu.VMEM((2, 2, GROUPS, 16, CH), BF),
-            pltpu.VMEM((2, 2, 4, 128, CH), BF),
+            pltpu.VMEM((2, 3, GROUPS, 16, CH), BF),
+            pltpu.VMEM((2, 3, 4, 128, CH), BF),
             pltpu.VMEM((GROUPS, CH * 8, 256), BF),
             pltpu.SemaphoreType.DMA((6, CHUNKS)),
             pltpu.SemaphoreType.DMA((5, CHUNKS)),

time: 92.4 us -> 89.5 us (0.969)
  Pallas kernels: 92.2 us -> 89.3 us
    pallas_call x1, Pallas kernels: 85.1 us -> 82.2 us  [exchange(): pl.pallas_call(exchange_kernel, out_shape=(pltpu.VMEM((CH // LAST, 2, NLA...]
where the time goes in v6:
time: 89.5 us; the launch traced here: 89.4 us
  Pallas kernels  89.3 us (100%)
    pallas_call x1, Pallas kernels, exchange(): pl.pallas_call(exchange_kernel, out_shape=(pltpu.VMEM((CH // LAST, 2, NLA...  82.2 us
    pallas_call x1, Pallas kernels, last(): pl.pallas_call(last_kernel, out_shape=jax.ShapeDtypeStruct((4, NLAG, CH,...  7.1 us

profile of v6, /device:TPU:16, one launch (start us, length us, event | category | flops | bytes accessed | tf_op | source)
XLA Modules:
  0.0 89.4 jit_solution(4969944426088971077)
XLA Ops:
  0.0 0.0 copy-start
  0.0 82.2 %exchange.1 = (f32[8,2,64,16,128]{4,3,2,1,0:T(8,128)S(1)}, bf16[128,256,256]{2,1,0:T(8,128)(2,1)S(1)}) custom-call(bf16[128,32768]{1,0:T(8,128)(2,1)} %record_ref.1, s32[1,128]{1,0:T(1,128)} %bitcast.2, bf16[544,1024]{1,0:T(8,128)(2,1)} %constant.8.clone.main_hbm, bf16[272,256]{1,0:T(8,128)(2,1)} %constant.9.clone.tail_hbm, ...), custom_call_target="tpu_custom_call" | custom-call | tf_op jit(solution)/shard_map/exchange/pallas_call | solution.py:516
  82.3 0.0 copy-done
  82.3 7.1 %last.1 = f32[4,64,128,128]{3,2,1,0:T(8,128)} custom-call(bf16[64,256]{1,0:T(8,128)(2,1)S(1)} %copy-done, f32[8,2,64,16,128]{4,3,2,1,0:T(8,128)S(1)} %get-tuple-element.7.near, bf16[128,256,256]{2,1,0:T(8,128)(2,1)S(1)} %get-tuple-element.8.far), custom_call_target="tpu_custom_call" | custom-call | tf_op jit(solution)/shard_map/last/pallas_call | solution.py:582
Async XLA Ops:
  0.0 82.3 %copy-start = (bf16[64,256]{1,0:T(8,128)(2,1)S(1)}, bf16[64,256]{1,0:T(8,128)(2,1)}, u32[]{:S(2)}) copy-start(bf16[64,256]{1,0:T(8,128)(2,1)} %constant.11.clone.lag_hbm.lag) | copy-start | bytes 98308

commit v7 on v6

--- a/solution.py
+++ b/solution.py
@@ -78,9 +78,10 @@
 PART = 32
 LENGTH = FRAMES * HALF
 LAST = 16
-
-
-KINDS = [2, 5, 6, 6, 3, 7, 6, 7, 4, 4, 2, 2, 5, 3, 3, 7]
+BUFFERS = 4
+
+
+KINDS = [5, 6, 6, 2, 2, 6, 3, 7, 7, 4, 2, 4, 5, 3, 7, 5]
 OWN = {
     0: {2: [("y", 1), ("z", 2)], 3: [("y", 1)], 4: [("y", 1)], 5: [("d", 4), ("y", 1)],
         6: [("y", 1), ("z", 2)], 7: [("d", 4), ("y", 1)]},
@@ -112,55 +113,63 @@
         [],
         [],
         [],
-        [(2, 0)],
-        [(4, 1)],
+        [(4, 0)],
+        [(2, 1)],
+        [],
         [],
         [(2, 2)],
-        [],
-        [(4, 5), (1, 0)],
+        [(5, 0), (1, 0)],
+        [],
         [(2, 3)],
-        [],
-        [(5, 1)],
-        [(1, 1), (2, 6)],
-        [(4, 7), (1, 2)],
+        [(4, 7)],
+        [(1, 1)],
+        [(2, 4), (2, 0), (1, 2)],
+        [],
+        [(2, 5)],
+        [(5, 7), (1, 3)],
         [(3, 0)],
-        [],
-        [],
-        [],
-        [(5, 5), (1, 3)],
+        [(4, 8)],
+        [(1, 4)],
         [(3, 1)],
-        [],
-        [],
-        [],
-        [(2, 1), (1, 4)],
+        [(4, 12)],
+        [(1, 5)],
         [(2, 10)],
-        [],
-        [],
-        [],
-        [(4, 12), (1, 5)],
-        [(2, 11), (4, 15), (1, 6), (3, 2), (5, 7), (1, 7), (3, 3), (2, 5), (1, 8)],
-        [(3, 4), (5, 12), (1, 9)],
-        [(3, 5), (5, 15), (1, 10)],
-        [(3, 6), (2, 7), (1, 11)],
-        [(3, 7), (2, 12), (1, 12)],
-        [(3, 8), (2, 15), (1, 13)],
-        [(3, 9), (1, 14)],
-        [(3, 10), (1, 15)],
+        [(4, 14), (1, 6)],
+        [(3, 2)],
+        [(4, 15)],
+        [(1, 7)],
+        [(3, 3)],
+        [(2, 7)],
+        [(1, 8)],
+        [(3, 4)],
+        [],
+        [(5, 8)],
+        [],
+        [(1, 9)],
+        [(3, 5)],
+        [],
+        [(5, 12)],
+        [(1, 10), (3, 6)],
+        [(5, 14), (1, 11)],
+        [(3, 7), (5, 15), (1, 12)],
+        [(3, 8), (2, 8), (1, 13)],
+        [(3, 9), (2, 12), (1, 14)],
+        [(3, 10), (2, 14), (1, 15)],
         [(3, 11)],
         [],
-        [],
-        [(2, 4), (3, 12)],
-        [],
-        [],
-        [(2, 8), (3, 13)],
-        [],
-        [],
-        [(2, 9), (3, 14)],
-        [],
-        [],
-        [(2, 13), (3, 15)],
-        [],
-        [(2, 14)],
+        [(2, 15)],
+        [],
+        [(2, 6)],
+        [(3, 12)],
+        [],
+        [],
+        [],
+        [(2, 9), (3, 13)],
+        [],
+        [(2, 11)],
+        [(3, 14)],
+        [(2, 13)],
+        [(3, 15)],
         [],
         [],
     ],
@@ -180,47 +189,55 @@
         [(1, 2), (2, 2)],
         [],
         [],
-        [(1, 3), (2, 3)],
+        [(4, 1), (1, 3), (2, 3)],
         [(4, 2)],
         [(1, 4), (2, 4)],
         [],
-        [],
-        [],
-        [(4, 3)],
-        [(1, 5), (2, 5)],
-        [],
-        [],
-        [],
-        [(5, 2)],
-        [(2, 6), (3, 0)],
-        [],
-        [],
-        [],
-        [(5, 3)],
-        [(1, 6), (2, 7), (3, 2), (1, 7), (2, 8), (3, 3), (1, 8), (2, 9)],
-        [(4, 6), (1, 9), (2, 10)],
-        [(4, 8), (1, 10), (2, 11)],
-        [(5, 6), (1, 11), (2, 12)],
-        [(4, 9), (1, 12), (2, 13)],
-        [(5, 8), (1, 13), (2, 14)],
-        [(3, 6), (1, 14), (2, 15)],
-        [(5, 9), (1, 15), (3, 4)],
-        [],
-        [],
-        [(3, 8), (3, 1), (3, 5)],
-        [],
-        [],
-        [(3, 9)],
-        [(3, 7), (3, 10)],
-        [],
-        [],
-        [(3, 11), (3, 13)],
+        [(5, 1), (1, 5), (2, 5)],
+        [],
+        [],
+        [(5, 2), (1, 6), (2, 6)],
+        [],
+        [(3, 1)],
+        [(1, 7), (2, 7)],
+        [],
+        [(4, 5), (2, 8), (3, 3)],
+        [],
+        [(3, 2)],
+        [(1, 8), (2, 9)],
+        [],
+        [(5, 5)],
+        [(1, 9), (2, 10)],
+        [],
+        [],
+        [],
+        [],
+        [(1, 10), (2, 11)],
+        [],
+        [],
+        [(3, 5)],
+        [(1, 11), (2, 12)],
+        [(4, 9)],
+        [(1, 12), (2, 13)],
+        [(4, 11), (1, 13), (2, 14)],
+        [(5, 9), (1, 14), (2, 15)],
+        [(5, 11), (1, 15), (3, 6)],
+        [],
+        [],
+        [],
+        [],
+        [(3, 9), (3, 4), (3, 7)],
+        [],
+        [],
+        [],
+        [(3, 11), (3, 0), (3, 8)],
+        [],
+        [(3, 10), (3, 13)],
         [],
         [(3, 12), (3, 14)],
         [],
         [],
         [(3, 15)],
-        [],
         [],
     ],
 )
@@ -238,12 +255,13 @@
     return sum(KINDS[c] in PASSING[parity] for c in range(first, chunk))
 
 
-def lags(lag, cross, which, target):
+def lags(lag, cross, which, target, rounds):
+    lanes = pl.ds(rounds[0] * CH, len(rounds) * CH)
     for j in range(LAST):
-        result = jnp.dot(lag[...], cross[which * LAST + j], preferred_element_type=F32)
-        for d in range(2):
+        result = jnp.dot(lag[...], cross[which * LAST + j, :, lanes], preferred_element_type=F32)
+        for i, d in enumerate(rounds):
             flat = target.at[d].reshape(NLAG * LAST, CH)
-            flat[pl.ds(j, NLAG, stride=LAST), :] = result[:, d * CH : (d + 1) * CH]
+            flat[pl.ds(j, NLAG, stride=LAST), :] = result[:, i * CH : (i + 1) * CH]
 
 
 def exchange_kernel(record_ref, quality_ref, main_hbm, tail_hbm, spread_hbm, lag_hbm, near_ref, far_ref,
@@ -449,54 +467,61 @@
     cols = lax.broadcasted_iota(jnp.int32, (PART * 8, 256), 1)
     diagonal = (rows % 4) == (cols % 4)
 
-    @pl.loop(0, GROUPS // 2)
-    def _(step):
-        visit(16, step, 16)
-        for j in range(2):
-            group = step * 2 + j
-            own = jnp.concatenate([white[group], turned[group]], 1)
-            for part in range(CH // PART):
-                lines = pl.ds(part * PART * 8, PART * 8)
-                table = lax.dot_general(spread[lines, :], own, NT, preferred_element_type=F32)
-                left[group, lines, :] = jnp.where(diagonal, table, 0.0).astype(BF)
-
-    def products(pair, one, two, store):
+    def fill(pair, table_of, rights, lanes):
         for part in range(CH // PART):
             lines = pl.ds(part * PART * 8, PART * 8)
             pieces = []
             for j in range(2):
                 group = 2 * pair + j
-                right = jnp.concatenate([one[group], two[group]], 1)
+                right = jnp.concatenate([ref[group] for ref in rights], 1)
                 pieces.append(
-                    jnp.dot(left[group, lines, :], right, preferred_element_type=F32).reshape(PART, 8, 2 * CH))
-            store(part, jnp.concatenate(pieces, 1).astype(BF))
-
-    def fill(which, one, two):
-        @pl.loop(0, 2)
-        def _(j):
-            pair = which * 2 + j
-
-            def store(part, value):
-                far_ref[pl.ds(part * PART, PART), pl.ds(pl.multiple_of(pair * 16, 16), 16), :] = value
-
-            products(pair, one, two, store)
+                    jnp.dot(table_of(group, lines), right, preferred_element_type=F32).reshape(
+                        PART, 8, len(rights) * CH))
+            far_ref[pl.ds(part * PART, PART), pl.ds(pl.multiple_of(pair * 16, 16), 16), lanes] = (
+                jnp.concatenate(pieces, 1).astype(BF))
+
+    def make_table(group, lines):
+        own = jnp.concatenate([white[group], turned[group]], 1)
+        table = lax.dot_general(spread[lines, :], own, NT, preferred_element_type=F32)
+        table = jnp.where(diagonal, table, 0.0).astype(BF)
+        left[group, lines, :] = table
+        return table
+
+    def load_table(group, lines):
+        return left[group, lines, :]
+
+    @pl.loop(0, GROUPS // 2)
+    def _(step):
+        visit(16, step, 16)
+        fill(step, make_table, [white], pl.ds(0, CH))
 
     @pl.loop(0, 8)
     def _(which):
         visit(32, which, 8)
-        fill(which, white, got.at[0])
+        lags(lag, far_ref, which, near_ref.at[which], (0,))
 
     @pl.loop(0, 8)
     def _(which):
         visit(40, which, 8)
-        lags(lag, far_ref, which, near_ref.at[which])
+
+        @pl.loop(0, 2)
+        def _(j):
+            fill(which * 2 + j, load_table, [got.at[0]], pl.ds(CH, CH))
 
     @pl.loop(0, 8)
     def _(which):
         visit(48, which, 8)
-        fill(which, got.at[1], got.at[2])
-
-    visit(56, 0, 1)
+        lags(lag, far_ref, which, near_ref.at[which], (1,))
+
+    @pl.loop(0, 8)
+    def _(which):
+        visit(56, which, 8)
+
+        @pl.loop(0, 2)
+        def _(j):
+            fill(which * 2 + j, load_table, [got.at[1], got.at[2]], pl.ds(0, 2 * CH))
+
+    visit(64, 0, 1)
 
     @on(segment > 0)
     def _():
@@ -531,8 +556,8 @@
             pltpu.VMEM((GROUPS, 256, CH), BF),
             pltpu.VMEM((GROUPS, 256, CH), BF),
             pltpu.VMEM((3, GROUPS, 256, CH), BF),
-            pltpu.VMEM((2, 3, GROUPS, 16, CH), BF),
-            pltpu.VMEM((2, 3, 4, 128, CH), BF),
+            pltpu.VMEM((2, 4, GROUPS, 16, CH), BF),
+            pltpu.VMEM((2, 4, 4, 128, CH), BF),
             pltpu.VMEM((GROUPS, CH * 8, 256), BF),
             pltpu.SemaphoreType.DMA((6, CHUNKS)),
             pltpu.SemaphoreType.DMA((5, CHUNKS)),
@@ -553,7 +578,7 @@
 
     def store_far(which):
         at = pl.ds(pl.multiple_of(which * LAST, LAST), LAST)
-        buffer = lax.rem(which, 2)
+        buffer = lax.rem(which, BUFFERS)
         return pltpu.make_async_copy(staged.at[buffer], out_ref.at[pl.ds(2, 2), :, at, :], far_sem.at[buffer])
 
     steps = CH // LAST
@@ -562,14 +587,14 @@
     def _(which):
         store_near(which).start()
 
-        @pl.when(which > 1)
+        @pl.when(which >= BUFFERS)
         def _():
-            store_far(which - 2).wait()
-
-        lags(lag, far, which, staged.at[lax.rem(which, 2)])
+            store_far(which - BUFFERS).wait()
+
+        lags(lag, far, which, staged.at[lax.rem(which, BUFFERS)], (0, 1))
         store_far(which).start()
 
-    for which in (steps - 2, steps - 1):
+    for which in range(steps - BUFFERS, steps):
         store_far(which).wait()
 
     @pl.loop(0, steps)
@@ -585,9 +610,9 @@
         in_specs=[inside] * 3,
         out_specs=pl.BlockSpec(memory_space=pl.ANY),
         scratch_shapes=[
-            pltpu.VMEM((2, 2, NLAG, LAST, CH), F32),
+            pltpu.VMEM((BUFFERS, 2, NLAG, LAST, CH), F32),
             pltpu.SemaphoreType.DMA((CH // LAST,)),
-            pltpu.SemaphoreType.DMA((2,)),
+            pltpu.SemaphoreType.DMA((BUFFERS,)),
         ],
         compiler_params=pltpu.CompilerParams(vmem_limit_bytes=8 * 2**20),
         name="last",

time: 89.5 us -> 88.1 us (0.984)
  Pallas kernels: 89.3 us -> 87.9 us
where the time goes in v7:
time: 88.1 us; the launch traced here: 88 us
  Pallas kernels  87.9 us (100%)
    pallas_call x1, Pallas kernels, exchange(): pl.pallas_call(exchange_kernel, out_shape=(pltpu.VMEM((CH // LAST, 2, NLA...  81.7 us
    pallas_call x1, Pallas kernels, last(): pl.pallas_call(last_kernel, out_shape=jax.ShapeDtypeStruct((4, NLAG, CH,...  6.21 us

profile of v7, /device:TPU:16, one launch (start us, length us, event | category | flops | bytes accessed | tf_op | source)
XLA Modules:
  0.0 88.0 jit_solution(15874625745732102545)
XLA Ops:
  0.0 0.0 copy-start
  0.0 81.7 %exchange.1 = (f32[8,2,64,16,128]{4,3,2,1,0:T(8,128)S(1)}, bf16[128,256,256]{2,1,0:T(8,128)(2,1)S(1)}) custom-call(bf16[128,32768]{1,0:T(8,128)(2,1)} %record_ref.1, s32[1,128]{1,0:T(1,128)} %bitcast.2, bf16[544,1024]{1,0:T(8,128)(2,1)} %constant.8.clone.main_hbm, bf16[272,256]{1,0:T(8,128)(2,1)} %constant.9.clone.tail_hbm, ...), custom_call_target="tpu_custom_call" | custom-call | tf_op jit(solution)/shard_map/exchange/pallas_call | solution.py:541
  81.7 0.0 copy-done
  81.8 6.2 %last.1 = f32[4,64,128,128]{3,2,1,0:T(8,128)} custom-call(bf16[64,256]{1,0:T(8,128)(2,1)S(1)} %copy-done, f32[8,2,64,16,128]{4,3,2,1,0:T(8,128)S(1)} %get-tuple-element.7.near, bf16[128,256,256]{2,1,0:T(8,128)(2,1)S(1)} %get-tuple-element.8.far), custom_call_target="tpu_custom_call" | custom-call | tf_op jit(solution)/shard_map/last/pallas_call | solution.py:607
Async XLA Ops:
  0.0 81.8 %copy-start = (bf16[64,256]{1,0:T(8,128)(2,1)S(1)}, bf16[64,256]{1,0:T(8,128)(2,1)}, u32[]{:S(2)}) copy-start(bf16[64,256]{1,0:T(8,128)(2,1)} %constant.11.clone.lag_hbm.lag) | copy-start | bytes 98308

commit v8 on v7

--- a/solution.py
+++ b/solution.py
@@ -280,10 +280,7 @@
     piece(0).start()
     tables[0].start()
     tables[1].start()
-    for i in range(1, FRAMES // 2):
-        piece(i).start()
-    tables[2].start()
-    tables[3].start()
+    piece(1).start()
 
     me = lax.axis_index("blk")
     count = lax.axis_size("blk")
@@ -395,6 +392,10 @@
     piece(0).wait()
     tables[0].wait()
     tables[1].wait()
+    for i in range(2, FRAMES // 2):
+        piece(i).start()
+    tables[2].start()
+    tables[3].start()
     held[...] = transform(rec[:, :HALF], rec[:, HALF : HALF + 128]).reshape(GROUPS + 2, 8, CH)
     keep = quality_ref[...].astype(F32).reshape(1, 1, CH)
 

time: 88.1 us -> 87 us (0.988)
  Pallas kernels: 87.9 us -> 86.8 us
    pallas_call x1, Pallas kernels: 81.7 us -> 80.6 us  [exchange(): pl.pallas_call(exchange_kernel, out_shape=(pltpu.VMEM((CH // LAST, 2, NLA...]
where the time goes in v8:
time: 87 us; the launch traced here: 86.9 us
  Pallas kernels  86.8 us (100%)
    pallas_call x1, Pallas kernels, exchange(): pl.pallas_call(exchange_kernel, out_shape=(pltpu.VMEM((CH // LAST, 2, NLA...  80.6 us
    pallas_call x1, Pallas kernels, last(): pl.pallas_call(last_kernel, out_shape=jax.ShapeDtypeStruct((4, NLAG, CH,...  6.21 us

profile of v8, /device:TPU:16, one launch (start us, length us, event | category | flops | bytes accessed | tf_op | source)
XLA Modules:
  0.0 86.9 jit_solution(6461783449086986763)
XLA Ops:
  0.0 0.0 copy-start
  0.0 80.6 %exchange.1 = (f32[8,2,64,16,128]{4,3,2,1,0:T(8,128)S(1)}, bf16[128,256,256]{2,1,0:T(8,128)(2,1)S(1)}) custom-call(bf16[128,32768]{1,0:T(8,128)(2,1)} %record_ref.1, s32[1,128]{1,0:T(1,128)} %bitcast.2, bf16[544,1024]{1,0:T(8,128)(2,1)} %constant.8.clone.main_hbm, bf16[272,256]{1,0:T(8,128)(2,1)} %constant.9.clone.tail_hbm, ...), custom_call_target="tpu_custom_call" | custom-call | tf_op jit(solution)/shard_map/exchange/pallas_call | solution.py:542
  80.6 0.0 copy-done
  80.6 6.2 %last.1 = f32[4,64,128,128]{3,2,1,0:T(8,128)} custom-call(bf16[64,256]{1,0:T(8,128)(2,1)S(1)} %copy-done, f32[8,2,64,16,128]{4,3,2,1,0:T(8,128)S(1)} %get-tuple-element.7.near, bf16[128,256,256]{2,1,0:T(8,128)(2,1)S(1)} %get-tuple-element.8.far), custom_call_target="tpu_custom_call" | custom-call | tf_op jit(solution)/shard_map/last/pallas_call | solution.py:608
Async XLA Ops:
  0.0 80.6 %copy-start = (bf16[64,256]{1,0:T(8,128)(2,1)S(1)}, bf16[64,256]{1,0:T(8,128)(2,1)}, u32[]{:S(2)}) copy-start(bf16[64,256]{1,0:T(8,128)(2,1)} %constant.11.clone.lag_hbm.lag) | copy-start | bytes 98308
